TPU v7x, 512 devices: a whole 4x8x8 slice. The times are simulated.
512 devices in a mesh: prow: 32 (over y, x), pcol: 16 (over z, core).
Axes of the slice: x: 4, y: 8, z: 8, core: 2. Of those that a mesh axis runs over, the one named last changes fastest.
Arguments:
- direction: float32 [3, 4096, 4096], P(None, 'prow', 'pcol'), may hold values from -6 to 6
- state: float32 [3, 4096, 4096], P(None, 'prow', 'pcol'), may hold values from -4 to 4
- material: int32 [4096, 4096], P('prow', 'pcol'), may hold values from 0 to 7
- trimmed: int32 [4096, 4096], P('prow', 'pcol'), may hold values 0 or 1
- moduli: float32 [8], replicated, may hold values from 0.5 to 4
- band: int32 [32, 16], P('prow', 'pcol'), may hold values from 64 to 256
- blocks: bfloat16 [32, 16, 3, 256, 256], P('prow', 'pcol')
- basis: bfloat16 [16, 4096, 4096], P(None, 'prow', 'pcol'), may hold values from -0.03125 to 0.03125
- coarse_inverse: float32 [48, 48], replicated
Outputs:
- product: float32 [3, 4096, 4096], P(None, 'prow', 'pcol')
All inputs are finite; a program needn't handle non-finite values. No bound on the sum of `trimmed` on one device may be relied on, other than what follows from the above.
Results may differ from a plain program's by a relative error of at most 0.0036.
Values may be sent and summed in bfloat16 or wider, within the bound.
A program may use at most 64 MiB of HBM per device.

v0:
```python
import jax
import jax.numpy as jnp
from jax import lax
from jax.sharding import PartitionSpec as P


def extended(cells, sides, width):
    for axis, dim in sides:
        count = lax.axis_size(axis)
        ends = count - 1
        head = lax.slice_in_dim(cells, 0, width, axis=dim)
        tail = lax.slice_in_dim(cells, cells.shape[dim] - width, cells.shape[dim], axis=dim)
        cells = jnp.concatenate(
            [
                lax.ppermute(tail, axis, [(i, (i + 1) % count) for i in range(ends)]),
                cells,
                lax.ppermute(head, axis, [((i + 1) % count, i) for i in range(ends)]),
            ],
            axis=dim,
        )
    return cells


def passed_along(shard, axis, by):
    length = lax.axis_size(axis)
    pairs = [(i, i + by) for i in range(length) if 0 <= i + by < length]
    return lax.ppermute(shard, axis, pairs)


def coefficients(state, material, trimmed, moduli):
    stretch = 1.0 + 0.3 * jnp.sum(state * state, axis=0)
    table = jnp.zeros(material.shape, jnp.float32)
    for entry in range(moduli.shape[0]):
        table = table + jnp.where(material == entry, moduli[entry], jnp.float32(0.0))
    return table * (stretch + 1.0 / stretch) * (0.25 + 0.75 * trimmed.astype(jnp.float32))


def tangent(padded, coef):
    centre = padded[:, 1:-1, 1:-1]
    beside = padded[:, 2:, 1:-1] + padded[:, :-2, 1:-1] + padded[:, 1:-1, 2:] + padded[:, 1:-1, :-2]
    coupled = jnp.roll(centre, -1, axis=0)
    return coef * (5.0 * centre - beside + 0.5 * coupled)


def body(direction, state, material, trimmed, moduli, band, blocks, basis, coarse_inverse):
    own_rows = direction.shape[1]
    own_cols = direction.shape[2]
    full_rows = blocks.shape[3]
    depth = (full_rows - own_rows) // 2
    coef = coefficients(state, material, trimmed, moduli)
    padded = extended(direction, (("prow", 1), ("pcol", 2)), 1)
    owned = tangent(padded, coef).astype(jnp.bfloat16)
    widened = extended(owned, (("prow", 1),), depth)
    flat_basis = basis.reshape(basis.shape[0], own_rows * own_cols)
    partial_sum = jnp.einsum(
        "cp,kp->ck",
        owned.reshape(3, own_rows * own_cols),
        flat_basis,
        preferred_element_type=jnp.float32,
    )
    coarse_sum = lax.psum(partial_sum, ("prow", "pcol"))
    span = jnp.arange(full_rows, dtype=jnp.int32)
    within = jnp.abs(span[:, None] - span[None, :]) <= band[0, 0]
    inverse = jnp.where(within[None], blocks[0, 0], jnp.zeros_like(blocks[0, 0]))
    local = jnp.einsum("cts,csj->ctj", inverse, widened, preferred_element_type=jnp.float32)
    omega = jnp.where((span < depth) | (span >= depth + own_rows), 0.5, 1.0).astype(jnp.float32)
    weighted = local * omega[None, :, None]
    from_above = passed_along(weighted[:, :depth].astype(jnp.bfloat16), "prow", -1).astype(
        jnp.float32
    )
    from_below = passed_along(
        weighted[:, depth + own_rows :].astype(jnp.bfloat16), "prow", 1
    ).astype(jnp.float32)
    assembled = weighted[:, depth : depth + own_rows]
    assembled = assembled + jnp.pad(from_below, ((0, 0), (0, own_rows - depth), (0, 0)))
    assembled = assembled + jnp.pad(from_above, ((0, 0), (own_rows - depth, 0), (0, 0)))
    coarse_step = jnp.dot(coarse_inverse, coarse_sum.reshape(-1), precision=lax.Precision.HIGHEST)
    coarse_step = coarse_step.reshape(3, basis.shape[0]).astype(jnp.bfloat16)
    coarse_term = jnp.dot(coarse_step, flat_basis, preferred_element_type=jnp.float32)
    return assembled + coarse_term.reshape(3, own_rows, own_cols)


def solution(mesh):
    placed = (
        P(None, "prow", "pcol"),
        P(None, "prow", "pcol"),
        P("prow", "pcol"),
        P("prow", "pcol"),
        P(),
        P("prow", "pcol"),
        P("prow", "pcol", None, None, None),
        P(None, "prow", "pcol"),
        P(),
    )
    return jax.shard_map(
        body, mesh=mesh, in_specs=placed, out_specs=P(None, "prow", "pcol"), check_vma=False
    )
```

profile of v0, /device:TPU:30, one launch (start us, length us, event | category | flops | bytes accessed | tf_op | source)
XLA Modules:
  0.0 152.0 jit_solution(8077264584084122307)
XLA Ops:
  0.0 0.8 fusion.29
  0.8 2.9 %collective-permute-start = (f32[3,1,256]{2,1,0:T(1,128)S(1)}, f32[3,1,256]{2,1,0:T(1,128)S(1)}, u32[]{:S(2)}, u32[]{:S(2)}) collective-permute-start(f32[3,1,256]{2,1,0:T(1,128)S(1)} %get-tuple-element.10), channel_id=1, source_target_pairs={{16,0},{32,16},{48,32},{64,48},{80,64},{96,80},{112,96},{128,112},... | collective-permute-start | bytes 9224 | tf_op jit(solution)/shard_map/ppermute | solution.py:17
  3.6 6.4 %collective-permute-start.1 = (f32[3,1,256]{2,1,0:T(1,128)S(1)}, f32[3,1,256]{2,1,0:T(1,128)S(1)}, u32[]{:S(2)}, u32[]{:S(2)}) collective-permute-start(f32[3,1,256]{2,1,0:T(1,128)S(1)} %get-tuple-element.9), channel_id=1, source_target_pairs={{0,16},{16,32},{32,48},{48,64},{64,80},{80,96},{96,112},{112,128},... | collective-permute-start | bytes 9224 | tf_op jit(solution)/shard_map/ppermute | solution.py:15
  10.1 0.7 fusion.31
  10.8 1.1 multiply_reduce_fusion
  12.6 5.2 %fusion.23 = f32[128,256]{1,0:T(8,128)S(1)} fusion(s32[128,256]{1,0:T(8,128)S(1)} %copy-done.3, f32[128,256]{1,0:T(8,128)S(1)} %multiply_reduce_fusion, s32[128,256]{1,0:T(8,128)S(1)} %copy-done.4, f32[]{:T(128)} %bitcast.9, f32[]{:T(128)} %bitcast.8, f32[]{:T(128)} %bitcast.7, f32[]{:T(128)} %bitcast.6, f32[]{:T(128)} %bitcast.5, f32[]{:T(128)} %bitcast.4, ...), kind=kLoop, calls=%fused_computation.41 | loop fusion | flops 1048576 | bytes 524320 | tf_op jit(solution)/shard_map/mul | solution.py:35
  18.0 0.1 fusion.27
  18.1 1.3 collective-permute-start.2
  19.4 3.0 %collective-permute-start.3 = (f32[3,130,1]{2,1,0:T(8,128)S(1)}, f32[3,130,1]{2,1,0:T(8,128)S(1)}, u32[]{:S(2)}, u32[]{:S(2)}) collective-permute-start(f32[3,130,1]{2,1,0:T(8,128)S(1)} %get-tuple-element.6), channel_id=1, source_target_pairs={{0,1},{1,2},{2,3},{3,4},{4,5},{5,6},{6,7},{7,8},{8,9},{9,10},{10,1... | collective-permute-start | bytes 4688 | tf_op jit(solution)/shard_map/ppermute | solution.py:15
  22.5 1.0 collective-permute-done.3
  23.5 0.2 slice-done
  23.8 0.4 fusion.11
  24.2 1.9 %collective-permute-start.4 = (bf16[3,64,256]{2,1,0:T(8,128)(2,1)S(1)}, bf16[3,64,256]{2,1,0:T(8,128)(2,1)S(1)}, u32[]{:S(2)}, u32[]{:S(2)}) collective-permute-start(bf16[3,64,256]{2,1,0:T(8,128)(2,1)S(1)} %get-tuple-element.11), channel_id=1, source_target_pairs={{0,16},{16,32},{32,48},{48,64},{64,80},{80,96},{96,112},{112,128},... | collective-permute-start | bytes 294920 | tf_op jit(solution)/shard_map/ppermute | solution.py:15
  26.1 4.1 %collective-permute-start.5 = (bf16[3,64,256]{2,1,0:T(8,128)(2,1)S(1)}, bf16[3,64,256]{2,1,0:T(8,128)(2,1)S(1)}, u32[]{:S(2)}, u32[]{:S(2)}) collective-permute-start(bf16[3,64,256]{2,1,0:T(8,128)(2,1)S(1)} %get-tuple-element.12), channel_id=1, source_target_pairs={{16,0},{32,16},{48,32},{64,48},{80,64},{96,80},{112,96},{128,112},... | collective-permute-start | bytes 294920 | tf_op jit(solution)/shard_map/ppermute | solution.py:17
  30.2 1.1 convolution_bitcast_fusion
  31.3 104.2 %psum.7 = f32[48]{0:T(128)S(1)} all-reduce(f32[48]{0:T(128)S(1)} %reshape.34), channel_id=1, replica_groups=mesh['prow'=32,'pcol'=16] {'prow','pcol'}, use_global_device_ids=true, to_apply=%region_1.2 | all-reduce | flops 48 | bytes 384 | tf_op jit(solution)/shard_map/psum | solution.py:61
  135.6 0.1 fusion
  135.7 0.1 reshape.39
  135.8 0.3 fusion.32
  136.1 5.2 %collective-permute-start.6 = (bf16[3,64,256]{2,1,0:T(8,128)(2,1)S(1)}, bf16[3,64,256]{2,1,0:T(8,128)(2,1)S(1)}, u32[]{:S(2)}, u32[]{:S(2)}) collective-permute-start(bf16[3,64,256]{2,1,0:T(8,128)(2,1)S(1)} %get-tuple-element.7), channel_id=1, source_target_pairs={{0,16},{16,32},{32,48},{48,64},{64,80},{80,96},{96,112},{112,128},... | collective-permute-start | bytes 294920 | tf_op jit(solution)/shard_map/ppermute | solution.py:27
  141.3 1.9 %collective-permute-start.7 = (bf16[3,64,256]{2,1,0:T(8,128)(2,1)S(1)}, bf16[3,64,256]{2,1,0:T(8,128)(2,1)S(1)}, u32[]{:S(2)}, u32[]{:S(2)}) collective-permute-start(bf16[3,64,256]{2,1,0:T(8,128)(2,1)S(1)} %get-tuple-element.8), channel_id=1, source_target_pairs={{16,0},{32,16},{48,32},{64,48},{80,64},{96,80},{112,96},{128,112},... | collective-permute-start | bytes 294920 | tf_op jit(solution)/shard_map/ppermute | solution.py:27
  143.2 0.7 fusion.1
  143.9 7.2 %collective-permute-done.7 = bf16[3,64,256]{2,1,0:T(8,128)(2,1)S(1)} collective-permute-done((bf16[3,64,256]{2,1,0:T(8,128)(2,1)S(1)}, bf16[3,64,256]{2,1,0:T(8,128)(2,1)S(1)}, u32[]{:S(2)}, u32[]{:S(2)}) %collective-permute-start.7) | collective-permute-done | bytes 98336 | tf_op jit(solution)/shard_map/ppermute | solution.py:27
  151.2 0.8 fusion.6
  (29 shorter events, 0.3 us)
Async XLA Ops:
  0.0 135.6 %copy-start = (f32[48,48]{1,0:T(8,128)S(1)}, f32[48,48]{1,0:T(8,128)}, u32[]{:S(2)}) copy-start(f32[48,48]{1,0:T(8,128)} %param.17) | copy-start | bytes 27652
  0.8 9.3 %copy-start.5 = (f32[8]{0:T(128)S(1)}, f32[8]{0:T(128)}, u32[]{:S(2)}) copy-start(f32[8]{0:T(128)} %param.13) | copy-start | bytes 100
  0.8 17.1 %collective-permute-start = (f32[3,1,256]{2,1,0:T(1,128)S(1)}, f32[3,1,256]{2,1,0:T(1,128)S(1)}, u32[]{:S(2)}, u32[]{:S(2)}) collective-permute-start(f32[3,1,256]{2,1,0:T(1,128)S(1)} %get-tuple-element.10), channel_id=1, source_target_pairs={{16,0},{32,16},{48,32},{64,48},{80,64},{96,80},{112,96},{128,112},... | collective-permute-start | bytes 9224 | tf_op jit(solution)/shard_map/ppermute | solution.py:17
  3.6 14.3 %collective-permute-start.1 = (f32[3,1,256]{2,1,0:T(1,128)S(1)}, f32[3,1,256]{2,1,0:T(1,128)S(1)}, u32[]{:S(2)}, u32[]{:S(2)}) collective-permute-start(f32[3,1,256]{2,1,0:T(1,128)S(1)} %get-tuple-element.9), channel_id=1, source_target_pairs={{0,16},{16,32},{32,48},{48,64},{64,80},{80,96},{96,112},{112,128},... | collective-permute-start | bytes 9224 | tf_op jit(solution)/shard_map/ppermute | solution.py:15
  10.8 1.8 %copy-start.3 = (s32[128,256]{1,0:T(8,128)S(1)}, s32[128,256]{1,0:T(8,128)}, u32[]{:S(2)}) copy-start(s32[128,256]{1,0:T(8,128)} %param.12) | copy-start | bytes 393220
  10.8 1.8 %copy-start.4 = (s32[128,256]{1,0:T(8,128)S(1)}, s32[128,256]{1,0:T(8,128)}, u32[]{:S(2)}) copy-start(s32[128,256]{1,0:T(8,128)} %param.11) | copy-start | bytes 393220
  11.9 6.1 %copy-start.1 = (f32[3,128,256]{2,1,0:T(8,128)S(1)}, f32[3,128,256]{2,1,0:T(8,128)}, u32[]{:S(2)}) copy-start(f32[3,128,256]{2,1,0:T(8,128)} %param.9) | copy-start | bytes 1179652
  18.1 4.4 %collective-permute-start.2 = (f32[3,130,1]{2,1,0:T(8,128)S(1)}, f32[3,130,1]{2,1,0:T(8,128)S(1)}, u32[]{:S(2)}, u32[]{:S(2)}) collective-permute-start(f32[3,130,1]{2,1,0:T(8,128)S(1)} %get-tuple-element.5), channel_id=1, source_target_pairs={{1,0},{2,1},{3,2},{4,3},{5,4},{6,5},{7,6},{8,7},{9,8},{10,9},{11,1... | collective-permute-start | bytes 4688 | tf_op jit(solution)/shard_map/ppermute | solution.py:17
  19.4 4.1 %collective-permute-start.3 = (f32[3,130,1]{2,1,0:T(8,128)S(1)}, f32[3,130,1]{2,1,0:T(8,128)S(1)}, u32[]{:S(2)}, u32[]{:S(2)}) collective-permute-start(f32[3,130,1]{2,1,0:T(8,128)S(1)} %get-tuple-element.6), channel_id=1, source_target_pairs={{0,1},{1,2},{2,3},{3,4},{4,5},{5,6},{6,7},{7,8},{8,9},{9,10},{10,1... | collective-permute-start | bytes 4688 | tf_op jit(solution)/shard_map/ppermute | solution.py:15
  22.5 1.3 slice-start
  22.5 1.3 slice-start.1
  22.5 7.7 %copy-start.2 = (bf16[16,128,256]{2,1,0:T(8,128)(2,1)S(1)}, bf16[16,128,256]{2,1,0:T(8,128)(2,1)}, u32[]{:S(2)}) copy-start(bf16[16,128,256]{2,1,0:T(8,128)(2,1)} %param.16) | copy-start | bytes 3145732
  24.2 111.6 %collective-permute-start.4 = (bf16[3,64,256]{2,1,0:T(8,128)(2,1)S(1)}, bf16[3,64,256]{2,1,0:T(8,128)(2,1)S(1)}, u32[]{:S(2)}, u32[]{:S(2)}) collective-permute-start(bf16[3,64,256]{2,1,0:T(8,128)(2,1)S(1)} %get-tuple-element.11), channel_id=1, source_target_pairs={{0,16},{16,32},{32,48},{48,64},{64,80},{80,96},{96,112},{112,128},... | collective-permute-start | bytes 294920 | tf_op jit(solution)/shard_map/ppermute | solution.py:15
  26.1 109.7 %copy-start.6 = (bf16[1,1,3,256,256]{4,3,2,1,0:T(8,128)(2,1)S(1)}, bf16[1,1,3,256,256]{4,3,2,1,0:T(8,128)(2,1)}, u32[]{:S(2)}) copy-start(bf16[1,1,3,256,256]{4,3,2,1,0:T(8,128)(2,1)} %param.15) | copy-start | bytes 1179652
  26.1 109.7 %collective-permute-start.5 = (bf16[3,64,256]{2,1,0:T(8,128)(2,1)S(1)}, bf16[3,64,256]{2,1,0:T(8,128)(2,1)S(1)}, u32[]{:S(2)}, u32[]{:S(2)}) collective-permute-start(bf16[3,64,256]{2,1,0:T(8,128)(2,1)S(1)} %get-tuple-element.12), channel_id=1, source_target_pairs={{16,0},{32,16},{48,32},{64,48},{80,64},{96,80},{112,96},{128,112},... | collective-permute-start | bytes 294920 | tf_op jit(solution)/shard_map/ppermute | solution.py:17
  136.1 7.8 %collective-permute-start.6 = (bf16[3,64,256]{2,1,0:T(8,128)(2,1)S(1)}, bf16[3,64,256]{2,1,0:T(8,128)(2,1)S(1)}, u32[]{:S(2)}, u32[]{:S(2)}) collective-permute-start(bf16[3,64,256]{2,1,0:T(8,128)(2,1)S(1)} %get-tuple-element.7), channel_id=1, source_target_pairs={{0,16},{16,32},{32,48},{48,64},{64,80},{80,96},{96,112},{112,128},... | collective-permute-start | bytes 294920 | tf_op jit(solution)/shard_map/ppermute | solution.py:27
  141.3 9.8 %collective-permute-start.7 = (bf16[3,64,256]{2,1,0:T(8,128)(2,1)S(1)}, bf16[3,64,256]{2,1,0:T(8,128)(2,1)S(1)}, u32[]{:S(2)}, u32[]{:S(2)}) collective-permute-start(bf16[3,64,256]{2,1,0:T(8,128)(2,1)S(1)} %get-tuple-element.8), channel_id=1, source_target_pairs={{16,0},{32,16},{48,32},{64,48},{80,64},{96,80},{112,96},{128,112},... | collective-permute-start | bytes 294920 | tf_op jit(solution)/shard_map/ppermute | solution.py:27
where the time goes:
time: 153 us; the launch traced here: 152 us
  blocking collectives  104 us (68%)
  starting transfers between devices  26.7 us (17%)
  waiting for transfers between devices  8.25 us (5%)
  other arithmetic  7.64 us (5%)
  matrix products  2.15 us (1%)
  local copies, waits for them, and re-layouts  2.07 us (1%)
    psum x1, blocking collectives, body(): coarse_sum = lax.psum(partial_sum, ('prow', 'pcol'))  104 us
    ppermute x3, starting transfers between devices, extended(): lax.ppermute(tail, axis, [(i, (i + 1) % count) for i in range(ends)])  11.4 us
    ppermute x3, starting transfers between devices, extended(): lax.ppermute(head, axis, [((i + 1) % count, i) for i in range(ends)])  8.21 us
    ppermute x2, waiting for transfers between devices, passed_along(): return lax.ppermute(shard, axis, pairs)  7.23 us
    ppermute x2, starting transfers between devices, passed_along(): return lax.ppermute(shard, axis, pairs)  7.08 us
    mul x1, other arithmetic, coefficients(): table * (stretch + 1.0 / stretch)  5.22 us
  transfers between devices with their start and end apart: 8, of which 2 were waited for; matrix products, arithmetic and copies ran while one was open for 6% of the time, Pallas kernels for 0%

commit v1 on v0

v1 whole, which is shorter than its diff:
```python
import functools

import jax
import jax.numpy as jnp
from jax import lax
from jax.experimental import pallas as pl
from jax.experimental.pallas import tpu as pltpu
from jax.sharding import PartitionSpec as P

MESH = pl.DeviceIdType.MESH
F32 = jnp.float32
BF16 = jnp.bfloat16
NT = (((1,), (1,)), ((), ()))
TN = (((0,), (0,)), ((), ()))


def iota(shape, dim):
    return lax.broadcasted_iota(jnp.int32, shape, dim)


def mm(a, b, dims=(((1,), (0,)), ((), ()))):
    return lax.dot_general(a, b, dims, preferred_element_type=F32)


def ones_where(cond):
    return jnp.where(cond, 1.0, 0.0).astype(BF16)


def kernel(
    nrow,
    ncol,
    dir_hbm,
    state_hbm,
    mat_hbm,
    trim_hbm,
    moduli_hbm,
    band_hbm,
    blocks_hbm,
    basis_hbm,
    inv_hbm,
    out_hbm,
    dpad,
    state,
    mat,
    trim,
    moduli,
    band,
    blk,
    basis,
    inv,
    coef,
    wide,
    own,
    outv,
    row_src,
    row_dst,
    col_src,
    col_dst,
    res_src,
    res_dst,
    sum1_src,
    sum1_dst,
    sum2_src,
    sum2_dst,
    irep,
    load_sem,
    out_sem,
    halo_ssem,
    halo_rsem,
    tan_ssem,
    tan_rsem,
    res_ssem,
    res_rsem,
    sum_ssem,
    sum_rsem,
):
    d = lax.axis_index("prow")
    e = lax.axis_index("pcol")
    up = (lax.rem(d + nrow - 1, nrow), e)
    down = (lax.rem(d + 1, nrow), e)
    left = (d, lax.rem(e + ncol - 1, ncol))
    right = (d, lax.rem(e + 1, ncol))
    rows, cols, ncoarse = 128, 256, 16
    groups = rows // 16

    def load(src, dst, i):
        copy = pltpu.make_async_copy(src, dst, load_sem.at[i])
        copy.start()
        return copy

    l_dir = load(dir_hbm, dpad.at[:, pl.ds(8, rows), :], 0)
    l_state = load(state_hbm, state, 1)
    l_mat = load(mat_hbm, mat, 2)
    l_trim = load(trim_hbm, trim, 3)
    l_mod = load(moduli_hbm, moduli, 4)
    l_basis = load(basis_hbm, basis, 5)
    l_blk = load(blocks_hbm.at[0, 0], blk, 6)
    l_band = load(band_hbm, band, 7)
    l_inv = load(inv_hbm, inv, 8)

    barrier = pltpu.get_barrier_semaphore()
    for k in range(1, ncol):
        pl.semaphore_signal(
            barrier, inc=1, device_id=(d, lax.rem(e + k, ncol)), device_id_type=MESH
        )
    for k in range(1, nrow):
        pl.semaphore_signal(
            barrier, inc=1, device_id=(lax.rem(d + k, nrow), e), device_id_type=MESH
        )

    def send(src, dst, ssem, rsem, to):
        copy = pltpu.make_async_remote_copy(
            src_ref=src, dst_ref=dst, send_sem=ssem, recv_sem=rsem, device_id=to, device_id_type=MESH
        )
        copy.start()
        return copy

    l_dir.wait()
    r16 = iota((16, cols), 0)
    c16 = iota((16, cols), 1)
    edge_cols = jnp.zeros((16, rows), F32)
    for c in range(3):
        pick = ones_where(((r16 == c) & (c16 == 0)) | ((r16 == 8 + c) & (c16 == cols - 1)))
        edge_cols = edge_cols + mm(pick, dpad[c, 8 : 8 + rows, :].astype(BF16), NT)
    col_src[...] = edge_cols
    row_src[...] = jnp.zeros_like(row_src)
    for c in range(3):
        row_src[0, c : c + 1, :] = dpad[c, 8:9, :]
        row_src[1, c : c + 1, :] = dpad[c, 7 + rows : 8 + rows, :]
    pl.semaphore_wait(barrier, ncol - 1 + nrow - 1)
    halo = [
        send(row_src.at[0], row_dst.at[1], halo_ssem.at[0], halo_rsem.at[0], up),
        send(row_src.at[1], row_dst.at[0], halo_ssem.at[1], halo_rsem.at[1], down),
        send(col_src.at[pl.ds(0, 8)], col_dst.at[pl.ds(8, 8)], halo_ssem.at[2], halo_rsem.at[2], left),
        send(col_src.at[pl.ds(8, 8)], col_dst.at[pl.ds(0, 8)], halo_ssem.at[3], halo_rsem.at[3], right),
    ]

    l_state.wait()
    l_mat.wait()
    l_trim.wait()
    l_mod.wait()
    for g in range(groups):
        at = slice(16 * g, 16 * g + 16)
        s0, s1, s2 = state[0, at, :], state[1, at, :], state[2, at, :]
        stretch = 1.0 + 0.3 * (s0 * s0 + s1 * s1 + s2 * s2)
        which = mat[at, :]
        table = jnp.full((16, cols), moduli[0], F32)
        for entry in range(1, 8):
            table = jnp.where(which == entry, moduli[entry], table)
        coef[at, :] = table * (stretch + 1.0 / stretch) * (0.25 + 0.75 * trim[at, :].astype(F32))

    for copy in halo:
        copy.wait_recv()
    row_in = iota((8, cols), 0)
    for c in range(3):
        above = jnp.where(d > 0, row_dst[0, c : c + 1, :], 0.0)
        below = jnp.where(d < nrow - 1, row_dst[1, c : c + 1, :], 0.0)
        dpad[c, 7:8, :] = above
        dpad[c, 8 + rows : 9 + rows, :] = below
    side = iota((16, rows), 0)
    keep = ((side < 8) & (e > 0)) | ((side >= 8) & (e < ncol - 1))
    edges = jnp.where(keep, col_dst[...], 0.0).astype(BF16)
    lane = iota((16, cols), 1)
    tan = []
    for c in range(3):
        place = ones_where(((r16 == c) & (c16 == 0)) | ((r16 == 8 + c) & (c16 == cols - 1)))
        sides = mm(edges, place, TN)
        for g in range(groups):
            r0 = 8 + 16 * g
            centre = dpad[c, r0 : r0 + 16, :]
            beside = dpad[c, r0 - 1 : r0 + 15, :] + dpad[c, r0 + 1 : r0 + 17, :]
            beside = beside + jnp.where(lane == 0, 0.0, pltpu.roll(centre, 1, 1))
            beside = beside + jnp.where(lane == cols - 1, 0.0, pltpu.roll(centre, cols - 1, 1))
            beside = beside + sides[16 * g : 16 * g + 16, :]
            coupled = dpad[(c + 1) % 3, r0 : r0 + 16, :]
            value = coef[16 * g : 16 * g + 16, :] * (5.0 * centre - beside + 0.5 * coupled)
            wide[c, 64 + 16 * g : 80 + 16 * g, :] = value.astype(BF16)
        tan.append(
            (
                send(wide.at[c, pl.ds(64, 64)], wide.at[c, pl.ds(192, 64)], tan_ssem.at[c, 0], tan_rsem.at[c, 0], up),
                send(wide.at[c, pl.ds(128, 64)], wide.at[c, pl.ds(0, 64)], tan_ssem.at[c, 1], tan_rsem.at[c, 1], down),
            )
        )

    l_basis.wait()
    acc = jnp.zeros((48, cols), F32)
    for g in range(groups):
        own_rows = wide[:, 64 + 16 * g : 80 + 16 * g, :].reshape(48, cols)
        functions = basis[:, 16 * g : 16 * g + 16, :].reshape(cols, cols)
        acc = acc + mm(own_rows, functions, NT)
    r48 = iota((48, cols), 0)
    c48 = iota((48, cols), 1)
    same = (r48 % 16) == (c48 % 16)
    acc = jnp.where(same, acc, 0.0)
    high = acc.astype(BF16)
    low = (acc - high.astype(F32)).astype(BF16)
    re = iota((cols, 128), 0)
    ce = iota((cols, 128), 1)
    fold = ones_where(((ce % 16) == (re // 16)) & (ce < 96))
    part = mm(high, fold) + mm(low, fold)
    rp = iota((48, 128), 0)
    cp = iota((48, 128), 1)
    part = jnp.where(((cp // 16) % 3) == (rp // 16), part, 0.0)
    part = jnp.sum(part, axis=0, keepdims=True)
    sum1_src[...] = part
    for k in range(1, ncol):
        send(sum1_src, sum1_dst.at[k - 1], sum_ssem.at[0], sum_rsem.at[0], (d, lax.rem(e + k, ncol)))

    l_blk.wait()
    l_band.wait()
    width = band[0, 0]
    for i in range(8):
        t = iota((32, 256), 0) + 32 * i
        s = iota((32, 256), 1)
        keep = jnp.abs(t - s) <= width
        keep = keep & ((s >= 64) | (d > 0)) & ((s < 192) | (d < nrow - 1))
        keep = keep & ((t >= 64) | (d > 0)) & ((t < 192) | (d < nrow - 1))
        factor = 0.5 if (i < 2 or i >= 6) else 1.0
        factor = jnp.where(keep, factor, 0.0).astype(BF16)
        for c in range(3):
            blk[c, 32 * i : 32 * i + 32, :] = blk[c, 32 * i : 32 * i + 32, :] * factor

    l_inv.wait()
    inv_high = inv[...].astype(BF16)
    inv_low = (inv[...] - inv_high.astype(F32)).astype(BF16)
    repeat = ones_where((iota((48, 768), 1) // 16) == iota((48, 768), 0))
    irep[0:48, :] = mm(inv_high, repeat, TN).astype(BF16)
    irep[48:96, :] = mm(inv_low, repeat, TN).astype(BF16)
    irep[96:128, :] = jnp.zeros((32, 768), BF16)

    def wait_sum(buf, stage):
        pltpu.make_async_remote_copy(
            src_ref=buf, dst_ref=buf, send_sem=sum_ssem.at[stage], recv_sem=sum_rsem.at[stage],
            device_id=right, device_id_type=MESH,
        ).wait()

    wait_sum(sum1_dst, 0)
    part = sum1_src[...] + jnp.sum(sum1_dst[...], axis=0)
    sum2_src[...] = part
    for k in range(1, nrow):
        send(sum2_src, sum2_dst.at[k - 1], sum_ssem.at[1], sum_rsem.at[1], (lax.rem(d + k, nrow), e))

    res = []
    for c in range(3):
        for copy in tan[c]:
            copy.wait()
        vec = wide[c]
        margins = mm(jnp.concatenate([blk[c, 0:64, :], blk[c, 192:256, :]], axis=0), vec)
        res_src[0, c] = margins[0:64, :].astype(BF16)
        res_src[1, c] = margins[64:128, :].astype(BF16)
        res.append(
            (
                send(res_src.at[0, c], res_dst.at[1, c], res_ssem.at[c, 0], res_rsem.at[c, 0], up),
                send(res_src.at[1, c], res_dst.at[0, c], res_ssem.at[c, 1], res_rsem.at[c, 1], down),
            )
        )
        own[c] = mm(blk[c, 64:192, :], vec)

    wait_sum(sum2_dst, 1)
    total = sum2_src[...] + jnp.sum(sum2_dst[...], axis=0)
    total = jnp.broadcast_to(total, (16, 128))
    high = total.astype(BF16).astype(F32)
    mid = (total - high).astype(BF16).astype(F32)
    low = total - high - mid
    rt = iota((16, 128), 0)
    split = jnp.where(rt == 0, high, jnp.where(rt == 1, mid, jnp.where(rt == 2, low, 0.0))).astype(BF16)
    step = jnp.sum(mm(split, irep[...]), axis=0, keepdims=True)
    step = step.astype(BF16).astype(F32)
    spread = jnp.concatenate(
        [jnp.broadcast_to(step[:, c * cols : c * cols + cols], (16, cols)) for c in range(3)], axis=0
    )
    spread = jnp.where(same, spread, 0.0).astype(BF16)
    for g in range(groups):
        functions = basis[:, 16 * g : 16 * g + 16, :].reshape(cols, cols)
        term = mm(spread, functions)
        for c in range(3):
            at = slice(16 * g, 16 * g + 16)
            own[c, at, :] = own[c, at, :] + term[16 * c : 16 * c + 16, :]

    writes = []
    for c in range(3):
        for copy in res[c]:
            copy.wait()
        outv[c, 0:64, :] = own[c, 0:64, :] + res_dst[0, c].astype(F32)
        outv[c, 64:128, :] = own[c, 64:128, :] + res_dst[1, c].astype(F32)
        copy = pltpu.make_async_copy(outv.at[c], out_hbm.at[c], out_sem.at[c])
        copy.start()
        writes.append(copy)
    for copy in halo:
        copy.wait_send()
    for copy in writes:
        copy.wait()


def body(nrow, ncol, *args):
    vm = pltpu.VMEM
    dma = pltpu.SemaphoreType.DMA
    return pl.pallas_call(
        functools.partial(kernel, nrow, ncol),
        out_shape=jax.ShapeDtypeStruct((3, 128, 256), F32),
        in_specs=[pl.BlockSpec(memory_space=pl.ANY)] * 9,
        out_specs=pl.BlockSpec(memory_space=pl.ANY),
        scratch_shapes=[
            vm((3, 144, 256), F32),
            vm((3, 128, 256), F32),
            vm((128, 256), jnp.int32),
            vm((128, 256), jnp.int32),
            pltpu.SMEM((8,), F32),
            pltpu.SMEM((1, 1), jnp.int32),
            vm((3, 256, 256), BF16),
            vm((16, 128, 256), BF16),
            vm((48, 48), F32),
            vm((128, 256), F32),
            vm((3, 256, 256), BF16),
            vm((3, 128, 256), F32),
            vm((3, 128, 256), F32),
            vm((2, 8, 256), F32),
            vm((2, 8, 256), F32),
            vm((16, 128), F32),
            vm((16, 128), F32),
            vm((2, 3, 64, 256), BF16),
            vm((2, 3, 64, 256), BF16),
            vm((1, 128), F32),
            vm((ncol - 1, 1, 128), F32),
            vm((1, 128), F32),
            vm((nrow - 1, 1, 128), F32),
            vm((128, 768), BF16),
            dma((9,)),
            dma((3,)),
            dma((4,)),
            dma((4,)),
            dma((3, 2)),
            dma((3, 2)),
            dma((3, 2)),
            dma((3, 2)),
            dma((2,)),
            dma((2,)),
        ],
        compiler_params=pltpu.CompilerParams(
            collective_id=0, has_side_effects=True, vmem_limit_bytes=40 * 1024 * 1024
        ),
        name="schwarz",
    )(*args)


def solution(mesh):
    placed = (
        P(None, "prow", "pcol"),
        P(None, "prow", "pcol"),
        P("prow", "pcol"),
        P("prow", "pcol"),
        P(),
        P("prow", "pcol"),
        P("prow", "pcol", None, None, None),
        P(None, "prow", "pcol"),
        P(),
    )
    return jax.shard_map(
        functools.partial(body, mesh.shape["prow"], mesh.shape["pcol"]),
        mesh=mesh,
        in_specs=placed,
        out_specs=P(None, "prow", "pcol"),
        check_vma=False,
    )
```

time: 153 us -> 42 us (0.27)
  the two profiles are of different devices: /device:TPU:30 before, /device:TPU:1 now
where the time goes in v1:
time: 42 us; the launch traced here: 41.6 us
  Pallas kernels  33.4 us (80%)
  local copies, waits for them, and re-layouts  7.5 us (18%)
  between operations  0.7 us (2%)
    pallas_call x1, Pallas kernels, body(): pl.pallas_call(functools.partial(kernel, nrow, ncol), out_shape=jax.Shape...  33.4 us
    unnamed x17, local copies, waits for them, and re-layouts  7.5 us

profile of v1, /device:TPU:1, one launch (start us, length us, event | category | flops | bytes accessed | tf_op | source)
XLA Modules:
  0.0 41.6 jit_solution(937246049015222941)
XLA Ops:
  0.0 0.0 copy-start.7
  0.7 0.0 copy-done.7
  0.7 0.0 copy-start
  0.7 1.2 %copy-done = bf16[16,128,256]{2,1,0:T(8,128)(2,1)S(1)} copy-done((bf16[16,128,256]{2,1,0:T(8,128)(2,1)S(1)}, bf16[16,128,256]{2,1,0:T(8,128)(2,1)}, u32[]{:S(2)}) %copy-start) | copy-done | bytes 1048600
  1.9 0.0 copy-start.1
  1.9 1.0 %copy-done.1 = f32[3,128,256]{2,1,0:T(8,128)S(1)} copy-done((f32[3,128,256]{2,1,0:T(8,128)S(1)}, f32[3,128,256]{2,1,0:T(8,128)}, u32[]{:S(2)}) %copy-start.1) | copy-done | bytes 393240
  2.9 0.0 copy-start.2
  2.9 1.0 %copy-done.2 = f32[3,128,256]{2,1,0:T(8,128)S(1)} copy-done((f32[3,128,256]{2,1,0:T(8,128)S(1)}, f32[3,128,256]{2,1,0:T(8,128)}, u32[]{:S(2)}) %copy-start.2) | copy-done | bytes 393240
  3.9 0.0 copy-start.3
  3.9 1.0 %copy-done.3 = bf16[1,1,3,256,256]{4,3,2,1,0:T(8,128)(2,1)S(1)} copy-done((bf16[1,1,3,256,256]{4,3,2,1,0:T(8,128)(2,1)S(1)}, bf16[1,1,3,256,256]{4,3,2,1,0:T(8,128)(2,1)}, u32[]{:S(2)}) %copy-start.3) | copy-done | bytes 393240
  4.9 0.0 copy-start.4
  4.9 0.9 %copy-done.4 = s32[128,256]{1,0:T(8,128)S(1)} copy-done((s32[128,256]{1,0:T(8,128)S(1)}, s32[128,256]{1,0:T(8,128)}, u32[]{:S(2)}) %copy-start.4) | copy-done | bytes 131096
  5.8 0.0 copy-start.5
  5.8 0.9 %copy-done.5 = s32[128,256]{1,0:T(8,128)S(1)} copy-done((s32[128,256]{1,0:T(8,128)S(1)}, s32[128,256]{1,0:T(8,128)}, u32[]{:S(2)}) %copy-start.5) | copy-done | bytes 131096
  6.7 0.0 copy-start.6
  6.7 0.7 %copy-done.6 = f32[48,48]{1,0:T(8,128)S(1)} copy-done((f32[48,48]{1,0:T(8,128)S(1)}, f32[48,48]{1,0:T(8,128)}, u32[]{:S(2)}) %copy-start.6) | copy-done | bytes 9240
  7.4 33.4 %schwarz.1 = f32[3,128,256]{2,1,0:T(8,128)S(1)} custom-call(f32[3,128,256]{2,1,0:T(8,128)S(1)} %copy-done.1, f32[3,128,256]{2,1,0:T(8,128)S(1)} %copy-done.2, s32[128,256]{1,0:T(8,128)S(1)} %copy-done.4, s32[128,256]{1,0:T(8,128)S(1)} %copy-done.5, f32[8]{0:T(128)S(1)} %copy-done.7, s32[1,1]{1,0:T(1,128)S(6)} %copy.11.band_hbm, ...), custom_call_target="tpu_custom_call" | custom-call | tf_op jit(solution)/shard_map/schwarz/pallas_call | solution.py:298
  40.9 0.7 %copy.12 = f32[3,128,256]{2,1,0:T(8,128)} copy(f32[3,128,256]{2,1,0:T(8,128)S(1)} %schwarz.1) | data formatting | bytes 786432
Async XLA Ops:
  0.0 0.7 %copy-start.7 = (f32[8]{0:T(128)S(1)}, f32[8]{0:T(128)}, u32[]{:S(2)}) copy-start(f32[8]{0:T(128)} %moduli_hbm.1) | copy-start | bytes 100
  0.7 1.2 %copy-start = (bf16[16,128,256]{2,1,0:T(8,128)(2,1)S(1)}, bf16[16,128,256]{2,1,0:T(8,128)(2,1)}, u32[]{:S(2)}) copy-start(bf16[16,128,256]{2,1,0:T(8,128)(2,1)} %basis_hbm.1) | copy-start | bytes 3145732
  1.9 1.0 %copy-start.1 = (f32[3,128,256]{2,1,0:T(8,128)S(1)}, f32[3,128,256]{2,1,0:T(8,128)}, u32[]{:S(2)}) copy-start(f32[3,128,256]{2,1,0:T(8,128)} %dir_hbm.1) | copy-start | bytes 1179652
  2.9 1.0 %copy-start.2 = (f32[3,128,256]{2,1,0:T(8,128)S(1)}, f32[3,128,256]{2,1,0:T(8,128)}, u32[]{:S(2)}) copy-start(f32[3,128,256]{2,1,0:T(8,128)} %state_hbm.1) | copy-start | bytes 1179652
  3.9 1.0 %copy-start.3 = (bf16[1,1,3,256,256]{4,3,2,1,0:T(8,128)(2,1)S(1)}, bf16[1,1,3,256,256]{4,3,2,1,0:T(8,128)(2,1)}, u32[]{:S(2)}) copy-start(bf16[1,1,3,256,256]{4,3,2,1,0:T(8,128)(2,1)} %blocks_hbm.1) | copy-start | bytes 1179652
  4.9 0.9 %copy-start.4 = (s32[128,256]{1,0:T(8,128)S(1)}, s32[128,256]{1,0:T(8,128)}, u32[]{:S(2)}) copy-start(s32[128,256]{1,0:T(8,128)} %mat_hbm.1) | copy-start | bytes 393220
  5.8 0.9 %copy-start.5 = (s32[128,256]{1,0:T(8,128)S(1)}, s32[128,256]{1,0:T(8,128)}, u32[]{:S(2)}) copy-start(s32[128,256]{1,0:T(8,128)} %trim_hbm.1) | copy-start | bytes 393220
  6.7 0.7 %copy-start.6 = (f32[48,48]{1,0:T(8,128)S(1)}, f32[48,48]{1,0:T(8,128)}, u32[]{:S(2)}) copy-start(f32[48,48]{1,0:T(8,128)} %inv_hbm.1) | copy-start | bytes 27652

commit v2 on v1

--- a/solution.py
+++ b/solution.py
@@ -24,6 +24,21 @@
 
 def ones_where(cond):
     return jnp.where(cond, 1.0, 0.0).astype(BF16)
+
+
+def far_first(n, dist):
+    return sorted(range(1, n), key=lambda k: (-dist(k), k))
+
+
+def ring(k, n):
+    return min(k % n, n - k % n)
+
+
+def prow_distance(k, n):
+    hops = 0
+    for x in range(4):
+        hops += ring((x + k) % 4 - x, 4) + ring((x + k) // 4, max(n // 4, 1))
+    return hops
 
 
 def kernel(
@@ -38,7 +53,7 @@
     blocks_hbm,
     basis_hbm,
     inv_hbm,
-    out_hbm,
+    out,
     dpad,
     state,
     mat,
@@ -51,8 +66,6 @@
     coef,
     wide,
     own,
-    outv,
-    row_src,
     row_dst,
     col_src,
     col_dst,
@@ -64,7 +77,6 @@
     sum2_dst,
     irep,
     load_sem,
-    out_sem,
     halo_ssem,
     halo_rsem,
     tan_ssem,
@@ -73,15 +85,27 @@
     res_rsem,
     sum_ssem,
     sum_rsem,
+    entry_sem,
 ):
     d = lax.axis_index("prow")
     e = lax.axis_index("pcol")
-    up = (lax.rem(d + nrow - 1, nrow), e)
-    down = (lax.rem(d + 1, nrow), e)
-    left = (d, lax.rem(e + ncol - 1, ncol))
-    right = (d, lax.rem(e + 1, ncol))
-    rows, cols, ncoarse = 128, 256, 16
+
+    def row_at(k):
+        return (lax.rem(d + (k + nrow) % nrow, nrow), e)
+
+    def col_at(k):
+        return (d, lax.rem(e + (k + ncol) % ncol, ncol))
+
+    up, down, left, right = row_at(-1), row_at(1), col_at(-1), col_at(1)
+    rows, cols = 128, 256
     groups = rows // 16
+
+    def signal(sem, to):
+        pl.semaphore_signal(sem, inc=1, device_id=to, device_id_type=MESH)
+
+    barrier = pltpu.get_barrier_semaphore()
+    for to in (up, down, left, right):
+        signal(barrier, to)
 
     def load(src, dst, i):
         copy = pltpu.make_async_copy(src, dst, load_sem.at[i])
@@ -93,20 +117,10 @@
     l_mat = load(mat_hbm, mat, 2)
     l_trim = load(trim_hbm, trim, 3)
     l_mod = load(moduli_hbm, moduli, 4)
-    l_basis = load(basis_hbm, basis, 5)
     l_blk = load(blocks_hbm.at[0, 0], blk, 6)
     l_band = load(band_hbm, band, 7)
     l_inv = load(inv_hbm, inv, 8)
-
-    barrier = pltpu.get_barrier_semaphore()
-    for k in range(1, ncol):
-        pl.semaphore_signal(
-            barrier, inc=1, device_id=(d, lax.rem(e + k, ncol)), device_id_type=MESH
-        )
-    for k in range(1, nrow):
-        pl.semaphore_signal(
-            barrier, inc=1, device_id=(lax.rem(d + k, nrow), e), device_id_type=MESH
-        )
+    l_basis = load(basis_hbm, basis, 5)
 
     def send(src, dst, ssem, rsem, to):
         copy = pltpu.make_async_remote_copy(
@@ -115,7 +129,31 @@
         copy.start()
         return copy
 
+    def tell(level):
+        step = 1 << level
+        sem = entry_sem.at[level]
+        count = 0
+        if step < nrow // 2:
+            signal(sem, row_at(step))
+            signal(sem, row_at(-step))
+            count += 2
+        if step < ncol // 2:
+            signal(sem, col_at(step))
+            signal(sem, col_at(-step))
+            count += 2
+        return count
+
+    def hear(level, count):
+        if count:
+            pl.semaphore_wait(entry_sem.at[level], count)
+
     l_dir.wait()
+    pl.semaphore_wait(barrier, 4)
+    halo = [
+        send(dpad.at[:, pl.ds(8, 8)], row_dst.at[1], halo_ssem.at[0], halo_rsem.at[0], up),
+        send(dpad.at[:, pl.ds(rows, 8)], row_dst.at[0], halo_ssem.at[1], halo_rsem.at[1], down),
+    ]
+    told = tell(0)
     r16 = iota((16, cols), 0)
     c16 = iota((16, cols), 1)
     edge_cols = jnp.zeros((16, rows), F32)
@@ -123,14 +161,7 @@
         pick = ones_where(((r16 == c) & (c16 == 0)) | ((r16 == 8 + c) & (c16 == cols - 1)))
         edge_cols = edge_cols + mm(pick, dpad[c, 8 : 8 + rows, :].astype(BF16), NT)
     col_src[...] = edge_cols
-    row_src[...] = jnp.zeros_like(row_src)
-    for c in range(3):
-        row_src[0, c : c + 1, :] = dpad[c, 8:9, :]
-        row_src[1, c : c + 1, :] = dpad[c, 7 + rows : 8 + rows, :]
-    pl.semaphore_wait(barrier, ncol - 1 + nrow - 1)
-    halo = [
-        send(row_src.at[0], row_dst.at[1], halo_ssem.at[0], halo_rsem.at[0], up),
-        send(row_src.at[1], row_dst.at[0], halo_ssem.at[1], halo_rsem.at[1], down),
+    halo += [
         send(col_src.at[pl.ds(0, 8)], col_dst.at[pl.ds(8, 8)], halo_ssem.at[2], halo_rsem.at[2], left),
         send(col_src.at[pl.ds(8, 8)], col_dst.at[pl.ds(0, 8)], halo_ssem.at[3], halo_rsem.at[3], right),
     ]
@@ -149,14 +180,40 @@
             table = jnp.where(which == entry, moduli[entry], table)
         coef[at, :] = table * (stretch + 1.0 / stretch) * (0.25 + 0.75 * trim[at, :].astype(F32))
 
+    hear(0, told)
+    told = tell(1)
+
+    l_blk.wait()
+    l_band.wait()
+    width = band[0, 0]
+    for i in range(8):
+        t = iota((32, 256), 0) + 32 * i
+        s = iota((32, 256), 1)
+        keep = jnp.abs(t - s) <= width
+        keep = keep & ((s >= 64) | (d > 0)) & ((s < 192) | (d < nrow - 1))
+        keep = keep & ((t >= 64) | (d > 0)) & ((t < 192) | (d < nrow - 1))
+        factor = 0.5 if (i < 2 or i >= 6) else 1.0
+        factor = jnp.where(keep, factor, 0.0).astype(BF16)
+        for c in range(3):
+            blk[c, 32 * i : 32 * i + 32, :] = blk[c, 32 * i : 32 * i + 32, :] * factor
+
+    l_inv.wait()
+    inv_high = inv[...].astype(BF16)
+    inv_low = (inv[...] - inv_high.astype(F32)).astype(BF16)
+    repeat = ones_where((iota((48, 768), 1) // 16) == iota((48, 768), 0))
+    irep[0:48, :] = mm(inv_high, repeat, TN).astype(BF16)
+    irep[48:96, :] = mm(inv_low, repeat, TN).astype(BF16)
+    irep[96:128, :] = jnp.zeros((32, 768), BF16)
+
+    hear(1, told)
+    told = tell(2)
+
+    l_basis.wait()
     for copy in halo:
         copy.wait_recv()
-    row_in = iota((8, cols), 0)
     for c in range(3):
-        above = jnp.where(d > 0, row_dst[0, c : c + 1, :], 0.0)
-        below = jnp.where(d < nrow - 1, row_dst[1, c : c + 1, :], 0.0)
-        dpad[c, 7:8, :] = above
-        dpad[c, 8 + rows : 9 + rows, :] = below
+        dpad[c, 7:8, :] = jnp.where(d > 0, row_dst[0, c, 7:8, :], 0.0)
+        dpad[c, 8 + rows : 9 + rows, :] = jnp.where(d < nrow - 1, row_dst[1, c, 0:1, :], 0.0)
     side = iota((16, rows), 0)
     keep = ((side < 8) & (e > 0)) | ((side >= 8) & (e < ncol - 1))
     edges = jnp.where(keep, col_dst[...], 0.0).astype(BF16)
@@ -182,7 +239,6 @@
             )
         )
 
-    l_basis.wait()
     acc = jnp.zeros((48, cols), F32)
     for g in range(groups):
         own_rows = wide[:, 64 + 16 * g : 80 + 16 * g, :].reshape(48, cols)
@@ -201,49 +257,23 @@
     rp = iota((48, 128), 0)
     cp = iota((48, 128), 1)
     part = jnp.where(((cp // 16) % 3) == (rp // 16), part, 0.0)
-    part = jnp.sum(part, axis=0, keepdims=True)
-    sum1_src[...] = part
-    for k in range(1, ncol):
-        send(sum1_src, sum1_dst.at[k - 1], sum_ssem.at[0], sum_rsem.at[0], (d, lax.rem(e + k, ncol)))
-
-    l_blk.wait()
-    l_band.wait()
-    width = band[0, 0]
-    for i in range(8):
-        t = iota((32, 256), 0) + 32 * i
-        s = iota((32, 256), 1)
-        keep = jnp.abs(t - s) <= width
-        keep = keep & ((s >= 64) | (d > 0)) & ((s < 192) | (d < nrow - 1))
-        keep = keep & ((t >= 64) | (d > 0)) & ((t < 192) | (d < nrow - 1))
-        factor = 0.5 if (i < 2 or i >= 6) else 1.0
-        factor = jnp.where(keep, factor, 0.0).astype(BF16)
-        for c in range(3):
-            blk[c, 32 * i : 32 * i + 32, :] = blk[c, 32 * i : 32 * i + 32, :] * factor
-
-    l_inv.wait()
-    inv_high = inv[...].astype(BF16)
-    inv_low = (inv[...] - inv_high.astype(F32)).astype(BF16)
-    repeat = ones_where((iota((48, 768), 1) // 16) == iota((48, 768), 0))
-    irep[0:48, :] = mm(inv_high, repeat, TN).astype(BF16)
-    irep[48:96, :] = mm(inv_low, repeat, TN).astype(BF16)
-    irep[96:128, :] = jnp.zeros((32, 768), BF16)
-
-    def wait_sum(buf, stage):
-        pltpu.make_async_remote_copy(
+    sum1_src[...] = jnp.sum(part, axis=0, keepdims=True)
+    hear(2, told)
+    told = tell(3)
+    for k in far_first(ncol, lambda k: ring(k, ncol)):
+        send(sum1_src, sum1_dst.at[k - 1], sum_ssem.at[0], sum_rsem.at[0], col_at(k))
+
+    def whole(buf, stage):
+        return pltpu.make_async_remote_copy(
             src_ref=buf, dst_ref=buf, send_sem=sum_ssem.at[stage], recv_sem=sum_rsem.at[stage],
             device_id=right, device_id_type=MESH,
-        ).wait()
-
-    wait_sum(sum1_dst, 0)
-    part = sum1_src[...] + jnp.sum(sum1_dst[...], axis=0)
-    sum2_src[...] = part
-    for k in range(1, nrow):
-        send(sum2_src, sum2_dst.at[k - 1], sum_ssem.at[1], sum_rsem.at[1], (lax.rem(d + k, nrow), e))
+        )
 
     res = []
-    for c in range(3):
+
+    def local(c):
         for copy in tan[c]:
-            copy.wait()
+            copy.wait_recv()
         vec = wide[c]
         margins = mm(jnp.concatenate([blk[c, 0:64, :], blk[c, 192:256, :]], axis=0), vec)
         res_src[0, c] = margins[0:64, :].astype(BF16)
@@ -256,7 +286,24 @@
         )
         own[c] = mm(blk[c, 64:192, :], vec)
 
-    wait_sum(sum2_dst, 1)
+    local(0)
+
+    whole(sum1_dst, 0).wait_recv()
+    sum2_src[...] = sum1_src[...] + jnp.sum(sum1_dst[...], axis=0)
+    hear(3, told)
+    for k in far_first(nrow, lambda k: prow_distance(k, nrow)):
+        send(sum2_src, sum2_dst.at[k - 1], sum_ssem.at[1], sum_rsem.at[1], row_at(k))
+
+    local(1)
+    local(2)
+
+    for c in range(3):
+        for copy in res[c]:
+            copy.wait_recv()
+        own[c, 0:64, :] = own[c, 0:64, :] + res_dst[0, c].astype(F32)
+        own[c, 64:128, :] = own[c, 64:128, :] + res_dst[1, c].astype(F32)
+
+    whole(sum2_dst, 1).wait_recv()
     total = sum2_src[...] + jnp.sum(sum2_dst[...], axis=0)
     total = jnp.broadcast_to(total, (16, 128))
     high = total.astype(BF16).astype(F32)
@@ -271,25 +318,17 @@
     )
     spread = jnp.where(same, spread, 0.0).astype(BF16)
     for g in range(groups):
-        functions = basis[:, 16 * g : 16 * g + 16, :].reshape(cols, cols)
-        term = mm(spread, functions)
+        at = slice(16 * g, 16 * g + 16)
+        term = mm(spread, basis[:, at, :].reshape(cols, cols))
         for c in range(3):
-            at = slice(16 * g, 16 * g + 16)
-            own[c, at, :] = own[c, at, :] + term[16 * c : 16 * c + 16, :]
-
-    writes = []
-    for c in range(3):
-        for copy in res[c]:
-            copy.wait()
-        outv[c, 0:64, :] = own[c, 0:64, :] + res_dst[0, c].astype(F32)
-        outv[c, 64:128, :] = own[c, 64:128, :] + res_dst[1, c].astype(F32)
-        copy = pltpu.make_async_copy(outv.at[c], out_hbm.at[c], out_sem.at[c])
-        copy.start()
-        writes.append(copy)
+            out[c, at, :] = own[c, at, :] + term[16 * c : 16 * c + 16, :]
     for copy in halo:
         copy.wait_send()
-    for copy in writes:
-        copy.wait()
+    for c in range(3):
+        for copy in tan[c] + res[c]:
+            copy.wait_send()
+    whole(sum1_dst, 0).wait_send()
+    whole(sum2_dst, 1).wait_send()
 
 
 def body(nrow, ncol, *args):
@@ -297,9 +336,9 @@
     dma = pltpu.SemaphoreType.DMA
     return pl.pallas_call(
         functools.partial(kernel, nrow, ncol),
-        out_shape=jax.ShapeDtypeStruct((3, 128, 256), F32),
-        in_specs=[pl.BlockSpec(memory_space=pl.ANY)] * 9,
-        out_specs=pl.BlockSpec(memory_space=pl.ANY),
+        out_shape=vm((3, 128, 256), F32),
+        in_specs=[pl.BlockSpec(memory_space=pltpu.HBM)] * 9,
+        out_specs=pl.BlockSpec(memory_space=vm),
         scratch_shapes=[
             vm((3, 144, 256), F32),
             vm((3, 128, 256), F32),
@@ -313,9 +352,7 @@
             vm((128, 256), F32),
             vm((3, 256, 256), BF16),
             vm((3, 128, 256), F32),
-            vm((3, 128, 256), F32),
-            vm((2, 8, 256), F32),
-            vm((2, 8, 256), F32),
+            vm((2, 3, 8, 256), F32),
             vm((16, 128), F32),
             vm((16, 128), F32),
             vm((2, 3, 64, 256), BF16),
@@ -326,7 +363,6 @@
             vm((nrow - 1, 1, 128), F32),
             vm((128, 768), BF16),
             dma((9,)),
-            dma((3,)),
             dma((4,)),
             dma((4,)),
             dma((3, 2)),
@@ -335,9 +371,10 @@
             dma((3, 2)),
             dma((2,)),
             dma((2,)),
+            pltpu.SemaphoreType.REGULAR((4,)),
         ],
         compiler_params=pltpu.CompilerParams(
-            collective_id=0, has_side_effects=True, vmem_limit_bytes=40 * 1024 * 1024
+            collective_id=0, has_side_effects=True, vmem_limit_bytes=56 * 1024 * 1024
         ),
         name="schwarz",
     )(*args)

time: 42 us -> 32.2 us (0.77)
  local copies, waits for them, and re-layouts: 7.5 us -> 0.75 us
  Pallas kernels: 33.4 us -> 30.6 us
    unnamed x17 -> x1, local copies, waits for them, and re-layouts: 7.5 us -> 0.75 us
    pallas_call x1, Pallas kernels: 33.4 us -> 30.6 us  [body(): pl.pallas_call(functools.partial(kernel, nrow, ncol), out_shape=vm((3, 12...]
where the time goes in v2:
time: 32.2 us; the launch traced here: 32 us
  Pallas kernels  30.6 us (95%)
  local copies, waits for them, and re-layouts  0.75 us (2%)
  between operations  0.66 us (2%)
    pallas_call x1, Pallas kernels, body(): pl.pallas_call(functools.partial(kernel, nrow, ncol), out_shape=vm((3, 12...  30.6 us
    unnamed x1, local copies, waits for them, and re-layouts  0.75 us

profile of v2, /device:TPU:1, one launch (start us, length us, event | category | flops | bytes accessed | tf_op | source)
XLA Modules:
  0.0 32.0 jit_solution(8044947038704371533)
XLA Ops:
  0.7 30.6 %schwarz.1 = f32[3,128,256]{2,1,0:T(8,128)S(1)} custom-call(f32[3,128,256]{2,1,0:T(8,128)} %dir_hbm.1, f32[3,128,256]{2,1,0:T(8,128)} %state_hbm.1, s32[128,256]{1,0:T(8,128)} %mat_hbm.1, s32[128,256]{1,0:T(8,128)} %trim_hbm.1, f32[8]{0:T(128)} %moduli_hbm.1, s32[1,1]{1,0:T(1,128)S(6)} %copy.12.band_hbm, bf16[1,1,3,256,256]{4,3,2,1,0:T(8,128)(2,1)} %blocks_hbm.1, ...), custom_call_target="tpu_custom_call" | custom-call | tf_op jit(solution)/shard_map/schwarz/pallas_call | solution.py:337
  31.3 0.7 %copy.11 = f32[3,128,256]{2,1,0:T(8,128)} copy(f32[3,128,256]{2,1,0:T(8,128)S(1)} %schwarz.1) | data formatting | bytes 786432

commit v3 on v2

--- a/solution.py
+++ b/solution.py
@@ -26,19 +26,45 @@
     return jnp.where(cond, 1.0, 0.0).astype(BF16)
 
 
-def far_first(n, dist):
-    return sorted(range(1, n), key=lambda k: (-dist(k), k))
-
-
 def ring(k, n):
     return min(k % n, n - k % n)
 
 
-def prow_distance(k, n):
-    hops = 0
-    for x in range(4):
-        hops += ring((x + k) % 4 - x, 4) + ring((x + k) // 4, max(n // 4, 1))
-    return hops
+def near_set(xs, ys, reach):
+    found = [(dx, dy) for dx in range(xs) for dy in range(ys) if 0 < ring(dx, xs) + ring(dy, ys) <= reach]
+    return sorted(found, key=lambda o: (ring(o[0], xs) + ring(o[1], ys), o))
+
+
+def sums_of(first, second, xs, ys):
+    second = set(second) | {(0, 0)}
+    return {((a + c) % xs, (b + f) % ys) for a, b in first for c, f in second}
+
+
+def entry_plan(xs, ys):
+    origin = {(0, 0)}
+    greet = {(dx % xs, dy % ys) for dx, dy in ((1, 0), (-1, 0), (0, 1), (0, -1), (1, 1), (-1, -1))} - origin
+    known = greet | origin
+    levels = []
+    while len(known) < xs * ys:
+        if not levels:
+            told = {(1 % xs, 0), (-1 % xs, 0), (0, 1 % ys), (0, -1 % ys)}
+        elif len(levels) == 1:
+            told = {(xs // 2, 0), (0, 2 % ys), (0, -2 % ys)}
+        else:
+            told = {(0, 2 % ys), (0, -2 % ys)}
+        told = sorted(told - origin)
+        levels.append(told)
+        known = sums_of(known, told, xs, ys)
+    return sorted(greet), levels
+
+
+def line_plan(n):
+    greet = [k for k in sorted(range(1, n), key=lambda k: (ring(k, n), k)) if ring(k, n) <= 2]
+    levels, reach = [], 2
+    while reach < n // 2:
+        levels.append([reach, n - reach])
+        reach *= 2
+    return greet, levels
 
 
 def kernel(
@@ -66,6 +92,7 @@
     coef,
     wide,
     own,
+    row_src,
     row_dst,
     col_src,
     col_dst,
@@ -76,11 +103,19 @@
     sum2_src,
     sum2_dst,
     irep,
+    place,
+    inner,
+    fix_src,
+    fix_dst,
+    edge_rows,
+    edge_functions,
     load_sem,
     halo_ssem,
     halo_rsem,
     tan_ssem,
     tan_rsem,
+    fix_ssem,
+    fix_rsem,
     res_ssem,
     res_rsem,
     sum_ssem,
@@ -90,22 +125,32 @@
     d = lax.axis_index("prow")
     e = lax.axis_index("pcol")
 
-    def row_at(k):
-        return (lax.rem(d + (k + nrow) % nrow, nrow), e)
-
     def col_at(k):
-        return (d, lax.rem(e + (k + ncol) % ncol, ncol))
-
-    up, down, left, right = row_at(-1), row_at(1), col_at(-1), col_at(1)
+        return (d, lax.rem(e + k % ncol, ncol))
+
+    xs, ys = 4, nrow // 4
+    x = lax.rem(d, xs)
+    y = d // xs
+
+    def row_at(offset):
+        dx, dy = offset
+        return (lax.rem(y + dy, ys) * xs + lax.rem(x + dx, xs), e)
+
+    up, down = (lax.rem(d + nrow - 1, nrow), e), (lax.rem(d + 1, nrow), e)
+    left, right = col_at(-1), col_at(1)
     rows, cols = 128, 256
     groups = rows // 16
 
     def signal(sem, to):
         pl.semaphore_signal(sem, inc=1, device_id=to, device_id_type=MESH)
 
+    row_greet, row_levels = entry_plan(xs, ys)
+    col_greet, col_levels = line_plan(ncol)
     barrier = pltpu.get_barrier_semaphore()
-    for to in (up, down, left, right):
-        signal(barrier, to)
+    for offset in row_greet:
+        signal(barrier, row_at(offset))
+    for k in col_greet:
+        signal(barrier, col_at(k))
 
     def load(src, dst, i):
         copy = pltpu.make_async_copy(src, dst, load_sem.at[i])
@@ -130,41 +175,38 @@
         return copy
 
     def tell(level):
-        step = 1 << level
-        sem = entry_sem.at[level]
         count = 0
-        if step < nrow // 2:
-            signal(sem, row_at(step))
-            signal(sem, row_at(-step))
-            count += 2
-        if step < ncol // 2:
-            signal(sem, col_at(step))
-            signal(sem, col_at(-step))
-            count += 2
+        for levels, at in ((row_levels, row_at), (col_levels, col_at)):
+            if level < len(levels):
+                for k in levels[level]:
+                    signal(entry_sem.at[level], at(k))
+                count += len(levels[level])
         return count
 
     def hear(level, count):
         if count:
             pl.semaphore_wait(entry_sem.at[level], count)
 
-    l_dir.wait()
-    pl.semaphore_wait(barrier, 4)
-    halo = [
-        send(dpad.at[:, pl.ds(8, 8)], row_dst.at[1], halo_ssem.at[0], halo_rsem.at[0], up),
-        send(dpad.at[:, pl.ds(rows, 8)], row_dst.at[0], halo_ssem.at[1], halo_rsem.at[1], down),
-    ]
-    told = tell(0)
     r16 = iota((16, cols), 0)
     c16 = iota((16, cols), 1)
+    l_dir.wait()
+    row_src[...] = jnp.zeros_like(row_src)
     edge_cols = jnp.zeros((16, rows), F32)
     for c in range(3):
+        row_src[0, c : c + 1, :] = dpad[c, 8:9, :]
+        row_src[1, c : c + 1, :] = dpad[c, 7 + rows : 8 + rows, :]
         pick = ones_where(((r16 == c) & (c16 == 0)) | ((r16 == 8 + c) & (c16 == cols - 1)))
+        place[c] = pick
         edge_cols = edge_cols + mm(pick, dpad[c, 8 : 8 + rows, :].astype(BF16), NT)
     col_src[...] = edge_cols
-    halo += [
+    pl.semaphore_wait(barrier, len(row_greet) + len(col_greet))
+    halo = [
+        send(row_src.at[0], row_dst.at[1], halo_ssem.at[0], halo_rsem.at[0], up),
+        send(row_src.at[1], row_dst.at[0], halo_ssem.at[1], halo_rsem.at[1], down),
         send(col_src.at[pl.ds(0, 8)], col_dst.at[pl.ds(8, 8)], halo_ssem.at[2], halo_rsem.at[2], left),
         send(col_src.at[pl.ds(8, 8)], col_dst.at[pl.ds(0, 8)], halo_ssem.at[3], halo_rsem.at[3], right),
     ]
+    told = tell(0)
 
     l_state.wait()
     l_mat.wait()
@@ -180,8 +222,94 @@
             table = jnp.where(which == entry, moduli[entry], table)
         coef[at, :] = table * (stretch + 1.0 / stretch) * (0.25 + 0.75 * trim[at, :].astype(F32))
 
+    lane = iota((16, cols), 1)
+    side = iota((16, cols), 0)
+    zero_row = jnp.zeros((1, cols), F32)
+    tan = []
+    for c in range(3):
+        dpad[c, 7:8, :] = zero_row
+        dpad[c, 8 + rows : 9 + rows, :] = zero_row
+        for g in range(groups):
+            r0 = 8 + 16 * g
+            at = slice(16 * g, 16 * g + 16)
+            centre = dpad[c, r0 : r0 + 16, :]
+            beside = dpad[c, r0 - 1 : r0 + 15, :] + dpad[c, r0 + 1 : r0 + 17, :]
+            beside = beside + jnp.where(lane == 0, 0.0, pltpu.roll(centre, 1, 1))
+            beside = beside + jnp.where(lane == cols - 1, 0.0, pltpu.roll(centre, cols - 1, 1))
+            coupled = dpad[(c + 1) % 3, r0 : r0 + 16, :]
+            value = coef[at, :] * (5.0 * centre - beside + 0.5 * coupled)
+            own[c, at, :] = value
+            inner[c, at, :] = value.astype(BF16)
+        tan.append(
+            (
+                send(inner.at[c, pl.ds(0, 64)], wide.at[c, pl.ds(192, 64)], tan_ssem.at[c, 0], tan_rsem.at[c, 0], up),
+                send(inner.at[c, pl.ds(64, 64)], wide.at[c, pl.ds(0, 64)], tan_ssem.at[c, 1], tan_rsem.at[c, 1], down),
+            )
+        )
+
+    coef_high = coef[...].astype(BF16)
+    coef_low = (coef[...] - coef_high.astype(F32)).astype(BF16)
+    both = ones_where(((r16 < 8) & (c16 == 0)) | ((r16 >= 8) & (c16 == cols - 1)))
+    coef_cols = mm(both, coef_high, NT) + mm(both, coef_low, NT)
+
     hear(0, told)
     told = tell(1)
+
+    halo[2].wait_recv()
+    halo[3].wait_recv()
+    half = iota((16, rows), 0)
+    keep = ((half < 8) & (e > 0)) | ((half >= 8) & (e < ncol - 1))
+    shares = -coef_cols * jnp.where(keep, col_dst[...], 0.0)
+    for i in range(2):
+        fix_src[i, 0:16, :] = shares
+        edge = coef[(rows - 1) * i : (rows - 1) * i + 1, :]
+        fix_src[i, 16:24, :] = jnp.concatenate(
+            [jnp.broadcast_to(edge[:, 0:128], (4, 128)), jnp.broadcast_to(edge[:, 128:256], (4, 128))], axis=0
+        )
+    fix = [
+        send(fix_src.at[0], fix_dst.at[1], fix_ssem.at[0], fix_rsem.at[0], up),
+        send(fix_src.at[1], fix_dst.at[0], fix_ssem.at[1], fix_rsem.at[1], down),
+    ]
+
+    l_basis.wait()
+    r48 = iota((48, cols), 0)
+    c48 = iota((48, cols), 1)
+    same = (r48 % 16) == (c48 % 16)
+    re = iota((cols, 128), 0)
+    ce = iota((cols, 128), 1)
+    fold = ones_where(((ce % 16) == (re // 16)) & (ce < 96))
+    rp = iota((48, 128), 0)
+    cp = iota((48, 128), 1)
+    rh = iota((16, 128), 0)
+    ch = iota((16, 128), 1)
+    mine = (((ch // 16) % 3) == (rh % 8)) & (rh % 8 < 3) & (ch < 96)
+
+    for c in range(3):
+        sides = mm(shares.astype(BF16), place[c], TN)
+        for g in range(groups):
+            at = slice(16 * g, 16 * g + 16)
+            value = own[c, at, :] + sides[at, :]
+            own[c, at, :] = value
+            wide[c, 64 + 16 * g : 80 + 16 * g, :] = value.astype(BF16)
+    acc = jnp.zeros((48, cols), F32)
+    for g in range(groups):
+        own_rows = wide[:, 64 + 16 * g : 80 + 16 * g, :].reshape(48, cols)
+        functions = basis[:, 16 * g : 16 * g + 16, :].reshape(cols, cols)
+        acc = acc + mm(own_rows, functions, NT)
+    acc = jnp.where(same, acc, 0.0)
+    high = acc.astype(BF16)
+    low = (acc - high.astype(F32)).astype(BF16)
+    part = mm(high, fold) + mm(low, fold)
+    part = jnp.where((((cp // 16) % 3) == (rp // 16)) & (cp < 96), part, 0.0)
+    sum1_src[...] = jnp.sum(part, axis=0, keepdims=True)
+    for k in range(16):
+        for i in range(2):
+            edge_rows[i, k : k + 1, :] = basis[k, (rows - 16) * i : (rows - 16) * i + 16, :].astype(F32)[15 * i : 15 * i + 1, :]
+    for i in range(2):
+        one = edge_rows[i].astype(BF16)
+        for j in range(6):
+            edge_functions[i, 16 * j : 16 * j + 16, :] = one
+        edge_functions[i, 96:128, :] = jnp.zeros((32, cols), BF16)
 
     l_blk.wait()
     l_band.wait()
@@ -208,60 +336,22 @@
     hear(1, told)
     told = tell(2)
 
-    l_basis.wait()
-    for copy in halo:
-        copy.wait_recv()
+    halo[0].wait_recv()
+    halo[1].wait_recv()
+    above = jnp.where(d > 0, row_dst[0], 0.0) * -coef[0:1, :]
+    below = jnp.where(d < nrow - 1, row_dst[1], 0.0) * -coef[rows - 1 : rows, :]
+    rim = jnp.concatenate([above, below], axis=0).astype(BF16)
+    part = jnp.where(rh < 8, mm(rim, edge_functions[0], NT), mm(rim, edge_functions[1], NT))
+    part = jnp.where(mine, part, 0.0)
+    sum1_src[...] = sum1_src[...] + jnp.sum(part, axis=0, keepdims=True)
+    for k in sorted(range(1, ncol), key=lambda k: (-ring(k, ncol), k)):
+        send(sum1_src, sum1_dst.at[k - 1], sum_ssem.at[0], sum_rsem.at[0], col_at(k))
+
     for c in range(3):
-        dpad[c, 7:8, :] = jnp.where(d > 0, row_dst[0, c, 7:8, :], 0.0)
-        dpad[c, 8 + rows : 9 + rows, :] = jnp.where(d < nrow - 1, row_dst[1, c, 0:1, :], 0.0)
-    side = iota((16, rows), 0)
-    keep = ((side < 8) & (e > 0)) | ((side >= 8) & (e < ncol - 1))
-    edges = jnp.where(keep, col_dst[...], 0.0).astype(BF16)
-    lane = iota((16, cols), 1)
-    tan = []
-    for c in range(3):
-        place = ones_where(((r16 == c) & (c16 == 0)) | ((r16 == 8 + c) & (c16 == cols - 1)))
-        sides = mm(edges, place, TN)
-        for g in range(groups):
-            r0 = 8 + 16 * g
-            centre = dpad[c, r0 : r0 + 16, :]
-            beside = dpad[c, r0 - 1 : r0 + 15, :] + dpad[c, r0 + 1 : r0 + 17, :]
-            beside = beside + jnp.where(lane == 0, 0.0, pltpu.roll(centre, 1, 1))
-            beside = beside + jnp.where(lane == cols - 1, 0.0, pltpu.roll(centre, cols - 1, 1))
-            beside = beside + sides[16 * g : 16 * g + 16, :]
-            coupled = dpad[(c + 1) % 3, r0 : r0 + 16, :]
-            value = coef[16 * g : 16 * g + 16, :] * (5.0 * centre - beside + 0.5 * coupled)
-            wide[c, 64 + 16 * g : 80 + 16 * g, :] = value.astype(BF16)
-        tan.append(
-            (
-                send(wide.at[c, pl.ds(64, 64)], wide.at[c, pl.ds(192, 64)], tan_ssem.at[c, 0], tan_rsem.at[c, 0], up),
-                send(wide.at[c, pl.ds(128, 64)], wide.at[c, pl.ds(0, 64)], tan_ssem.at[c, 1], tan_rsem.at[c, 1], down),
-            )
-        )
-
-    acc = jnp.zeros((48, cols), F32)
-    for g in range(groups):
-        own_rows = wide[:, 64 + 16 * g : 80 + 16 * g, :].reshape(48, cols)
-        functions = basis[:, 16 * g : 16 * g + 16, :].reshape(cols, cols)
-        acc = acc + mm(own_rows, functions, NT)
-    r48 = iota((48, cols), 0)
-    c48 = iota((48, cols), 1)
-    same = (r48 % 16) == (c48 % 16)
-    acc = jnp.where(same, acc, 0.0)
-    high = acc.astype(BF16)
-    low = (acc - high.astype(F32)).astype(BF16)
-    re = iota((cols, 128), 0)
-    ce = iota((cols, 128), 1)
-    fold = ones_where(((ce % 16) == (re // 16)) & (ce < 96))
-    part = mm(high, fold) + mm(low, fold)
-    rp = iota((48, 128), 0)
-    cp = iota((48, 128), 1)
-    part = jnp.where(((cp // 16) % 3) == (rp // 16), part, 0.0)
-    sum1_src[...] = jnp.sum(part, axis=0, keepdims=True)
-    hear(2, told)
-    told = tell(3)
-    for k in far_first(ncol, lambda k: ring(k, ncol)):
-        send(sum1_src, sum1_dst.at[k - 1], sum_ssem.at[0], sum_rsem.at[0], col_at(k))
+        first = own[c, 0:16, :] + jnp.where(side == 0, above[c : c + 1, :], 0.0)
+        last = own[c, rows - 16 : rows, :] + jnp.where(side == 15, below[c : c + 1, :], 0.0)
+        wide[c, 64:80, :] = first.astype(BF16)
+        wide[c, 48 + rows : 64 + rows, :] = last.astype(BF16)
 
     def whole(buf, stage):
         return pltpu.make_async_remote_copy(
@@ -274,6 +364,20 @@
     def local(c):
         for copy in tan[c]:
             copy.wait_recv()
+        if c == 0:
+            for copy in fix:
+                copy.wait_recv()
+        for i in range(2):
+            sides = mm(fix_dst[i, 0:16, :].astype(BF16), place[c], TN)
+            edge = jnp.concatenate([fix_dst[i, 16:17, :], fix_dst[i, 20:21, :]], axis=1)
+            beyond = dpad[c, 8:9, :] if i == 0 else dpad[c, 7 + rows : 8 + rows, :]
+            for j in range(4):
+                to = slice(192 * i + 16 * j, 192 * i + 16 * j + 16)
+                lines = slice(64 * (1 - i) + 16 * j, 64 * (1 - i) + 16 * j + 16)
+                value = wide[c, to, :].astype(F32) + sides[lines, :]
+                if j == (3 if i == 0 else 0):
+                    value = value - jnp.where(side == (15 if i == 0 else 0), edge * beyond, 0.0)
+                wide[c, to, :] = value.astype(BF16)
         vec = wide[c]
         margins = mm(jnp.concatenate([blk[c, 0:64, :], blk[c, 192:256, :]], axis=0), vec)
         res_src[0, c] = margins[0:64, :].astype(BF16)
@@ -290,9 +394,10 @@
 
     whole(sum1_dst, 0).wait_recv()
     sum2_src[...] = sum1_src[...] + jnp.sum(sum1_dst[...], axis=0)
-    hear(3, told)
-    for k in far_first(nrow, lambda k: prow_distance(k, nrow)):
-        send(sum2_src, sum2_dst.at[k - 1], sum_ssem.at[1], sum_rsem.at[1], row_at(k))
+    hear(2, told)
+    for offset in reversed(near_set(xs, ys, nrow)):
+        slot = offset[1] * xs + offset[0] - 1
+        send(sum2_src, sum2_dst.at[slot], sum_ssem.at[1], sum_rsem.at[1], row_at(offset))
 
     local(1)
     local(2)
@@ -322,7 +427,7 @@
         term = mm(spread, basis[:, at, :].reshape(cols, cols))
         for c in range(3):
             out[c, at, :] = own[c, at, :] + term[16 * c : 16 * c + 16, :]
-    for copy in halo:
+    for copy in halo + fix:
         copy.wait_send()
     for c in range(3):
         for copy in tan[c] + res[c]:
@@ -352,7 +457,8 @@
             vm((128, 256), F32),
             vm((3, 256, 256), BF16),
             vm((3, 128, 256), F32),
-            vm((2, 3, 8, 256), F32),
+            vm((2, 8, 256), F32),
+            vm((2, 8, 256), F32),
             vm((16, 128), F32),
             vm((16, 128), F32),
             vm((2, 3, 64, 256), BF16),
@@ -362,16 +468,24 @@
             vm((1, 128), F32),
             vm((nrow - 1, 1, 128), F32),
             vm((128, 768), BF16),
+            vm((3, 16, 256), BF16),
+            vm((3, 128, 256), BF16),
+            vm((2, 24, 128), F32),
+            vm((2, 24, 128), F32),
+            vm((2, 16, 256), F32),
+            vm((2, 128, 256), BF16),
             dma((9,)),
             dma((4,)),
             dma((4,)),
             dma((3, 2)),
             dma((3, 2)),
+            dma((2,)),
+            dma((2,)),
             dma((3, 2)),
             dma((3, 2)),
             dma((2,)),
             dma((2,)),
-            pltpu.SemaphoreType.REGULAR((4,)),
+            pltpu.SemaphoreType.REGULAR((3,)),
         ],
         compiler_params=pltpu.CompilerParams(
             collective_id=0, has_side_effects=True, vmem_limit_bytes=56 * 1024 * 1024

time: 32.2 us -> 30.1 us (0.935)
  Pallas kernels: 30.6 us -> 28.6 us
    pallas_call x1, Pallas kernels: 30.6 us -> 28.6 us  [body(): pl.pallas_call(functools.partial(kernel, nrow, ncol), out_shape=vm((3, 12...]
where the time goes in v3:
time: 30.1 us; the launch traced here: 30 us
  Pallas kernels  28.6 us (95%)
  local copies, waits for them, and re-layouts  0.75 us (2%)
  between operations  0.66 us (2%)
    pallas_call x1, Pallas kernels, body(): pl.pallas_call(functools.partial(kernel, nrow, ncol), out_shape=vm((3, 12...  28.6 us
    unnamed x1, local copies, waits for them, and re-layouts  0.75 us

profile of v3, /device:TPU:1, one launch (start us, length us, event | category | flops | bytes accessed | tf_op | source)
XLA Modules:
  0.0 30.0 jit_solution(14465959633938026485)
XLA Ops:
  0.7 28.6 %schwarz.1 = f32[3,128,256]{2,1,0:T(8,128)S(1)} custom-call(f32[3,128,256]{2,1,0:T(8,128)} %dir_hbm.1, f32[3,128,256]{2,1,0:T(8,128)} %state_hbm.1, s32[128,256]{1,0:T(8,128)} %mat_hbm.1, s32[128,256]{1,0:T(8,128)} %trim_hbm.1, f32[8]{0:T(128)} %moduli_hbm.1, s32[1,1]{1,0:T(1,128)S(6)} %copy.12.band_hbm, bf16[1,1,3,256,256]{4,3,2,1,0:T(8,128)(2,1)} %blocks_hbm.1, ...), custom_call_target="tpu_custom_call" | custom-call | tf_op jit(solution)/shard_map/schwarz/pallas_call | solution.py:442
  29.2 0.7 %copy.11 = f32[3,128,256]{2,1,0:T(8,128)} copy(f32[3,128,256]{2,1,0:T(8,128)S(1)} %schwarz.1) | data formatting | bytes 786432

commit v4 on v3

--- a/solution.py
+++ b/solution.py
@@ -35,36 +35,37 @@
     return sorted(found, key=lambda o: (ring(o[0], xs) + ring(o[1], ys), o))
 
 
-def sums_of(first, second, xs, ys):
-    second = set(second) | {(0, 0)}
-    return {((a + c) % xs, (b + f) % ys) for a, b in first for c, f in second}
-
-
-def entry_plan(xs, ys):
-    origin = {(0, 0)}
-    greet = {(dx % xs, dy % ys) for dx, dy in ((1, 0), (-1, 0), (0, 1), (0, -1), (1, 1), (-1, -1))} - origin
-    known = greet | origin
-    levels = []
-    while len(known) < xs * ys:
+def row_plan(xs, ys):
+    def shift(p, q):
+        return ((p[0] + q[0]) % xs, (p[1] + q[1]) % ys)
+
+    def offsets(pairs):
+        return {shift((0, 0), p) for p in pairs} - {(0, 0)}
+
+    first = offsets([(1, 0), (0, -1)])
+    known, levels = set(first), []
+    while len(known) < xs * ys - 1:
         if not levels:
-            told = {(1 % xs, 0), (-1 % xs, 0), (0, 1 % ys), (0, -1 % ys)}
+            told = first
         elif len(levels) == 1:
-            told = {(xs // 2, 0), (0, 2 % ys), (0, -2 % ys)}
+            told = set(known)
         else:
-            told = {(0, 2 % ys), (0, -2 % ys)}
-        told = sorted(told - origin)
-        levels.append(told)
-        known = sums_of(known, told, xs, ys)
-    return sorted(greet), levels
+            told = offsets([(0, 2), (0, -2)])
+        assert told <= known
+        back = offsets([(-p[0], -p[1]) for p in told])
+        known = known | back | {shift(p, q) for p in back for q in known}
+        known.discard((0, 0))
+        levels.append(sorted(told))
+    return sorted(first), levels
 
 
 def line_plan(n):
-    greet = [k for k in sorted(range(1, n), key=lambda k: (ring(k, n), k)) if ring(k, n) <= 2]
+    first = [k for k in range(1, n) if ring(k, n) <= 2]
     levels, reach = [], 2
     while reach < n // 2:
-        levels.append([reach, n - reach])
+        levels.append(sorted({reach, n - reach}))
         reach *= 2
-    return greet, levels
+    return first, levels
 
 
 def kernel(
@@ -108,7 +109,8 @@
     fix_src,
     fix_dst,
     edge_rows,
-    edge_functions,
+    rim_src,
+    rim_dst,
     load_sem,
     halo_ssem,
     halo_rsem,
@@ -116,6 +118,8 @@
     tan_rsem,
     fix_ssem,
     fix_rsem,
+    rim_ssem,
+    rim_rsem,
     res_ssem,
     res_rsem,
     sum_ssem,
@@ -144,13 +148,8 @@
     def signal(sem, to):
         pl.semaphore_signal(sem, inc=1, device_id=to, device_id_type=MESH)
 
-    row_greet, row_levels = entry_plan(xs, ys)
-    col_greet, col_levels = line_plan(ncol)
-    barrier = pltpu.get_barrier_semaphore()
-    for offset in row_greet:
-        signal(barrier, row_at(offset))
-    for k in col_greet:
-        signal(barrier, col_at(k))
+    row_first, row_levels = row_plan(xs, ys)
+    col_first, col_levels = line_plan(ncol)
 
     def load(src, dst, i):
         copy = pltpu.make_async_copy(src, dst, load_sem.at[i])
@@ -158,14 +157,21 @@
         return copy
 
     l_dir = load(dir_hbm, dpad.at[:, pl.ds(8, rows), :], 0)
+    barrier = pltpu.get_barrier_semaphore()
+    for dx, dy in row_first:
+        signal(barrier, row_at((-dx % xs, -dy % ys)))
+    for k in col_first:
+        signal(barrier, col_at(-k))
     l_state = load(state_hbm, state, 1)
     l_mat = load(mat_hbm, mat, 2)
     l_trim = load(trim_hbm, trim, 3)
     l_mod = load(moduli_hbm, moduli, 4)
+    last = rows - 16
+    l_ends = [load(basis_hbm.at[:, pl.ds(r, 16)], basis.at[:, pl.ds(r, 16)], i) for r, i in ((0, 9), (last, 10))]
+    l_basis = load(basis_hbm.at[:, pl.ds(16, rows - 32)], basis.at[:, pl.ds(16, rows - 32)], 5)
     l_blk = load(blocks_hbm.at[0, 0], blk, 6)
     l_band = load(band_hbm, band, 7)
     l_inv = load(inv_hbm, inv, 8)
-    l_basis = load(basis_hbm, basis, 5)
 
     def send(src, dst, ssem, rsem, to):
         copy = pltpu.make_async_remote_copy(
@@ -199,15 +205,6 @@
         place[c] = pick
         edge_cols = edge_cols + mm(pick, dpad[c, 8 : 8 + rows, :].astype(BF16), NT)
     col_src[...] = edge_cols
-    pl.semaphore_wait(barrier, len(row_greet) + len(col_greet))
-    halo = [
-        send(row_src.at[0], row_dst.at[1], halo_ssem.at[0], halo_rsem.at[0], up),
-        send(row_src.at[1], row_dst.at[0], halo_ssem.at[1], halo_rsem.at[1], down),
-        send(col_src.at[pl.ds(0, 8)], col_dst.at[pl.ds(8, 8)], halo_ssem.at[2], halo_rsem.at[2], left),
-        send(col_src.at[pl.ds(8, 8)], col_dst.at[pl.ds(0, 8)], halo_ssem.at[3], halo_rsem.at[3], right),
-    ]
-    told = tell(0)
-
     l_state.wait()
     l_mat.wait()
     l_trim.wait()
@@ -222,10 +219,36 @@
             table = jnp.where(which == entry, moduli[entry], table)
         coef[at, :] = table * (stretch + 1.0 / stretch) * (0.25 + 0.75 * trim[at, :].astype(F32))
 
+    for copy in l_ends:
+        copy.wait()
+    for i in range(2):
+        edge = coef[(rows - 1) * i : (rows - 1) * i + 1, :]
+        for k in range(16):
+            line = basis[k, last * i : last * i + 16, :].astype(F32)[15 * i : 15 * i + 1, :]
+            edge_rows[i, k : k + 1, :] = line * edge
+        rim_src[i, 0:16, :] = jnp.concatenate([row_src[1 * i], jnp.zeros((8, cols), F32)], axis=0).astype(BF16)
+        rim_src[i, 16:32, :] = edge_rows[i].astype(BF16)
+    pl.semaphore_wait(barrier, len(row_first) + len(col_first))
+    halo = [
+        send(col_src.at[pl.ds(0, 8)], col_dst.at[pl.ds(8, 8)], halo_ssem.at[2], halo_rsem.at[2], left),
+        send(col_src.at[pl.ds(8, 8)], col_dst.at[pl.ds(0, 8)], halo_ssem.at[3], halo_rsem.at[3], right),
+    ]
+    told = tell(0)
+
+    rim_up = pltpu.make_async_remote_copy(
+        src_ref=rim_src.at[0], dst_ref=rim_dst.at[0], send_sem=rim_ssem.at[0], recv_sem=rim_rsem.at[0],
+        device_id=row_at((0, ys - 1)), device_id_type=MESH,
+    )
+
+    @pl.when(x == 0)
+    def _():
+        rim_up.start()
+
+    rim_right = send(rim_src.at[1], rim_dst.at[1], rim_ssem.at[1], rim_rsem.at[1], row_at((1, 0)))
+
     lane = iota((16, cols), 1)
     side = iota((16, cols), 0)
     zero_row = jnp.zeros((1, cols), F32)
-    tan = []
     for c in range(3):
         dpad[c, 7:8, :] = zero_row
         dpad[c, 8 + rows : 9 + rows, :] = zero_row
@@ -240,6 +263,20 @@
             value = coef[at, :] * (5.0 * centre - beside + 0.5 * coupled)
             own[c, at, :] = value
             inner[c, at, :] = value.astype(BF16)
+
+    coef_high = coef[...].astype(BF16)
+    coef_low = (coef[...] - coef_high.astype(F32)).astype(BF16)
+    both = ones_where(((r16 < 8) & (c16 == 0)) | ((r16 >= 8) & (c16 == cols - 1)))
+    coef_cols = mm(both, coef_high, NT) + mm(both, coef_low, NT)
+
+    hear(0, told)
+    told = tell(1)
+    halo += [
+        send(row_src.at[0], row_dst.at[1], halo_ssem.at[0], halo_rsem.at[0], up),
+        send(row_src.at[1], row_dst.at[0], halo_ssem.at[1], halo_rsem.at[1], down),
+    ]
+    tan = []
+    for c in range(3):
         tan.append(
             (
                 send(inner.at[c, pl.ds(0, 64)], wide.at[c, pl.ds(192, 64)], tan_ssem.at[c, 0], tan_rsem.at[c, 0], up),
@@ -247,19 +284,48 @@
             )
         )
 
-    coef_high = coef[...].astype(BF16)
-    coef_low = (coef[...] - coef_high.astype(F32)).astype(BF16)
-    both = ones_where(((r16 < 8) & (c16 == 0)) | ((r16 >= 8) & (c16 == cols - 1)))
-    coef_cols = mm(both, coef_high, NT) + mm(both, coef_low, NT)
-
-    hear(0, told)
-    told = tell(1)
-
-    halo[2].wait_recv()
-    halo[3].wait_recv()
+    l_basis.wait()
+    r48 = iota((48, cols), 0)
+    c48 = iota((48, cols), 1)
+    same = (r48 % 16) == (c48 % 16)
+    re = iota((cols, 128), 0)
+    ce = iota((cols, 128), 1)
+    fold = ones_where(((ce % 16) == (re // 16)) & (ce < 96))
+    rp = iota((48, 128), 0)
+    cp = iota((48, 128), 1)
+    acc = jnp.zeros((48, cols), F32)
+    for g in range(groups):
+        own_rows = inner[:, 16 * g : 16 * g + 16, :].reshape(48, cols)
+        functions = basis[:, 16 * g : 16 * g + 16, :].reshape(cols, cols)
+        acc = acc + mm(own_rows, functions, NT)
+    acc = jnp.where(same, acc, 0.0)
+    high = acc.astype(BF16)
+    low = (acc - high.astype(F32)).astype(BF16)
+    part = mm(high, fold) + mm(low, fold)
+    part = jnp.where((((cp // 16) % 3) == (rp // 16)) & (cp < 96), part, 0.0)
+    sum1_src[...] = jnp.sum(part, axis=0, keepdims=True)
+
+    rb = iota((cols, cols), 0)
+    cb = iota((cols, cols), 1)
+    ends = ones_where(((rb == 0) & (cb < 128)) | ((rb == cols - 1) & (cb >= 128)))
+    lb = iota((rows, cols), 1)
+    edge_basis = jnp.zeros((rows, cols), F32)
+    for k in range(16):
+        edge_basis = jnp.where(lb % 16 == k, mm(basis[k], ends), edge_basis)
+    edge_basis = edge_basis.astype(BF16)
+
+    halo[0].wait_recv()
+    halo[1].wait_recv()
     half = iota((16, rows), 0)
     keep = ((half < 8) & (e > 0)) | ((half >= 8) & (e < ncol - 1))
     shares = -coef_cols * jnp.where(keep, col_dst[...], 0.0)
+    shares_low = shares.astype(BF16)
+    rh = iota((16, 128), 0)
+    ch = iota((16, 128), 1)
+    part = jnp.where(rh < 8, mm(shares_low, edge_basis[:, 0:128]), mm(shares_low, edge_basis[:, 128:256]))
+    part = jnp.where(((ch // 16) % 3 == rh % 8) & (rh % 8 < 3) & (ch < 96), part, 0.0)
+    sum1_src[...] = sum1_src[...] + jnp.sum(part, axis=0, keepdims=True)
+
     for i in range(2):
         fix_src[i, 0:16, :] = shares
         edge = coef[(rows - 1) * i : (rows - 1) * i + 1, :]
@@ -271,45 +337,27 @@
         send(fix_src.at[1], fix_dst.at[0], fix_ssem.at[1], fix_rsem.at[1], down),
     ]
 
-    l_basis.wait()
-    r48 = iota((48, cols), 0)
-    c48 = iota((48, cols), 1)
-    same = (r48 % 16) == (c48 % 16)
-    re = iota((cols, 128), 0)
-    ce = iota((cols, 128), 1)
-    fold = ones_where(((ce % 16) == (re // 16)) & (ce < 96))
-    rp = iota((48, 128), 0)
-    cp = iota((48, 128), 1)
-    rh = iota((16, 128), 0)
-    ch = iota((16, 128), 1)
-    mine = (((ch // 16) % 3) == (rh % 8)) & (rh % 8 < 3) & (ch < 96)
-
-    for c in range(3):
-        sides = mm(shares.astype(BF16), place[c], TN)
-        for g in range(groups):
-            at = slice(16 * g, 16 * g + 16)
-            value = own[c, at, :] + sides[at, :]
-            own[c, at, :] = value
-            wide[c, 64 + 16 * g : 80 + 16 * g, :] = value.astype(BF16)
-    acc = jnp.zeros((48, cols), F32)
-    for g in range(groups):
-        own_rows = wide[:, 64 + 16 * g : 80 + 16 * g, :].reshape(48, cols)
-        functions = basis[:, 16 * g : 16 * g + 16, :].reshape(cols, cols)
-        acc = acc + mm(own_rows, functions, NT)
-    acc = jnp.where(same, acc, 0.0)
-    high = acc.astype(BF16)
-    low = (acc - high.astype(F32)).astype(BF16)
-    part = mm(high, fold) + mm(low, fold)
-    part = jnp.where((((cp // 16) % 3) == (rp // 16)) & (cp < 96), part, 0.0)
-    sum1_src[...] = jnp.sum(part, axis=0, keepdims=True)
-    for k in range(16):
-        for i in range(2):
-            edge_rows[i, k : k + 1, :] = basis[k, (rows - 16) * i : (rows - 16) * i + 16, :].astype(F32)[15 * i : 15 * i + 1, :]
-    for i in range(2):
-        one = edge_rows[i].astype(BF16)
-        for j in range(6):
-            edge_functions[i, 16 * j : 16 * j + 16, :] = one
-        edge_functions[i, 96:128, :] = jnp.zeros((32, cols), BF16)
+    @pl.when(x == 0)
+    def _():
+        rim_up.wait_recv()
+
+    @pl.when(x != 0)
+    def _():
+        rim_dst[0] = rim_src[0]
+
+    rim_right.wait_recv()
+    upper = rim_dst[1]
+    lower = rim_dst[0]
+    values = jnp.concatenate([upper[0:16, :], lower[0:16, :]], axis=1)
+    edge = jnp.concatenate([lower[16:32, :], upper[16:32, :]], axis=1)
+    edge = jnp.concatenate([edge] * 6 + [jnp.zeros((32, 2 * cols), BF16)], axis=0)
+    inside = (x > 0) | (y < ys - 1)
+    part = jnp.where(((ch // 16) % 3 == rh) & (ch < 96) & inside, mm(values, edge, NT), 0.0)
+    sum1_src[...] = sum1_src[...] - jnp.sum(part, axis=0, keepdims=True)
+    hear(1, told)
+    told = tell(2)
+    for k in sorted(range(1, ncol), key=lambda k: (-ring(k, ncol), k)):
+        send(sum1_src, sum1_dst.at[k - 1], sum_ssem.at[0], sum_rsem.at[0], col_at(k))
 
     l_blk.wait()
     l_band.wait()
@@ -333,25 +381,20 @@
     irep[48:96, :] = mm(inv_low, repeat, TN).astype(BF16)
     irep[96:128, :] = jnp.zeros((32, 768), BF16)
 
-    hear(1, told)
-    told = tell(2)
-
-    halo[0].wait_recv()
-    halo[1].wait_recv()
+    halo[2].wait_recv()
+    halo[3].wait_recv()
     above = jnp.where(d > 0, row_dst[0], 0.0) * -coef[0:1, :]
     below = jnp.where(d < nrow - 1, row_dst[1], 0.0) * -coef[rows - 1 : rows, :]
-    rim = jnp.concatenate([above, below], axis=0).astype(BF16)
-    part = jnp.where(rh < 8, mm(rim, edge_functions[0], NT), mm(rim, edge_functions[1], NT))
-    part = jnp.where(mine, part, 0.0)
-    sum1_src[...] = sum1_src[...] + jnp.sum(part, axis=0, keepdims=True)
-    for k in sorted(range(1, ncol), key=lambda k: (-ring(k, ncol), k)):
-        send(sum1_src, sum1_dst.at[k - 1], sum_ssem.at[0], sum_rsem.at[0], col_at(k))
-
-    for c in range(3):
-        first = own[c, 0:16, :] + jnp.where(side == 0, above[c : c + 1, :], 0.0)
-        last = own[c, rows - 16 : rows, :] + jnp.where(side == 15, below[c : c + 1, :], 0.0)
-        wide[c, 64:80, :] = first.astype(BF16)
-        wide[c, 48 + rows : 64 + rows, :] = last.astype(BF16)
+    for c in range(3):
+        sides = mm(shares_low, place[c], TN)
+        for g in range(groups):
+            at = slice(16 * g, 16 * g + 16)
+            value = own[c, at, :] + sides[at, :]
+            if g == 0:
+                value = value + jnp.where(side == 0, above[c : c + 1, :], 0.0)
+            if g == groups - 1:
+                value = value + jnp.where(side == 15, below[c : c + 1, :], 0.0)
+            wide[c, 64 + 16 * g : 80 + 16 * g, :] = value.astype(BF16)
 
     def whole(buf, stage):
         return pltpu.make_async_remote_copy(
@@ -388,7 +431,6 @@
                 send(res_src.at[1, c], res_dst.at[0, c], res_ssem.at[c, 1], res_rsem.at[c, 1], down),
             )
         )
-        own[c] = mm(blk[c, 64:192, :], vec)
 
     local(0)
 
@@ -402,6 +444,8 @@
     local(1)
     local(2)
 
+    for c in range(3):
+        own[c] = mm(blk[c, 64:192, :], wide[c])
     for c in range(3):
         for copy in res[c]:
             copy.wait_recv()
@@ -427,8 +471,13 @@
         term = mm(spread, basis[:, at, :].reshape(cols, cols))
         for c in range(3):
             out[c, at, :] = own[c, at, :] + term[16 * c : 16 * c + 16, :]
-    for copy in halo + fix:
+    for copy in halo + fix + [rim_right]:
         copy.wait_send()
+
+    @pl.when(x == 0)
+    def _():
+        rim_up.wait_send()
+
     for c in range(3):
         for copy in tan[c] + res[c]:
             copy.wait_send()
@@ -473,12 +522,15 @@
             vm((2, 24, 128), F32),
             vm((2, 24, 128), F32),
             vm((2, 16, 256), F32),
-            vm((2, 128, 256), BF16),
-            dma((9,)),
+            vm((2, 32, 256), BF16),
+            vm((2, 32, 256), BF16),
+            dma((11,)),
             dma((4,)),
             dma((4,)),
             dma((3, 2)),
             dma((3, 2)),
+            dma((2,)),
+            dma((2,)),
             dma((2,)),
             dma((2,)),
             dma((3, 2)),

time: 30.1 us -> 29.2 us (0.970)
  Pallas kernels: 28.6 us -> 27.6 us
    pallas_call x1, Pallas kernels: 28.6 us -> 27.6 us  [body(): pl.pallas_call(functools.partial(kernel, nrow, ncol), out_shape=vm((3, 12...]
where the time goes in v4:
time: 29.2 us; the launch traced here: 29.1 us
  Pallas kernels  27.6 us (95%)
  local copies, waits for them, and re-layouts  0.75 us (3%)
  between operations  0.66 us (2%)
    pallas_call x1, Pallas kernels, body(): pl.pallas_call(functools.partial(kernel, nrow, ncol), out_shape=vm((3, 12...  27.6 us
    unnamed x1, local copies, waits for them, and re-layouts  0.75 us

profile of v4, /device:TPU:1, one launch (start us, length us, event | category | flops | bytes accessed | tf_op | source)
XLA Modules:
  0.0 29.1 jit_solution(14421512771456682984)
XLA Ops:
  0.7 27.6 %schwarz.1 = f32[3,128,256]{2,1,0:T(8,128)S(1)} custom-call(f32[3,128,256]{2,1,0:T(8,128)} %dir_hbm.1, f32[3,128,256]{2,1,0:T(8,128)} %state_hbm.1, s32[128,256]{1,0:T(8,128)} %mat_hbm.1, s32[128,256]{1,0:T(8,128)} %trim_hbm.1, f32[8]{0:T(128)} %moduli_hbm.1, s32[1,1]{1,0:T(1,128)S(6)} %copy.12.band_hbm, bf16[1,1,3,256,256]{4,3,2,1,0:T(8,128)(2,1)} %blocks_hbm.1, ...), custom_call_target="tpu_custom_call" | custom-call | tf_op jit(solution)/shard_map/schwarz/pallas_call | solution.py:491
  28.3 0.7 %copy.11 = f32[3,128,256]{2,1,0:T(8,128)} copy(f32[3,128,256]{2,1,0:T(8,128)S(1)} %schwarz.1) | data formatting | bytes 786432

commit v5 on v4

--- a/solution.py
+++ b/solution.py
@@ -60,8 +60,8 @@
 
 
 def line_plan(n):
-    first = [k for k in range(1, n) if ring(k, n) <= 2]
-    levels, reach = [], 2
+    first = [k for k in range(1, n) if ring(k, n) <= 4]
+    levels, reach = [], 4
     while reach < n // 2:
         levels.append(sorted({reach, n - reach}))
         reach *= 2
@@ -182,7 +182,7 @@
 
     def tell(level):
         count = 0
-        for levels, at in ((row_levels, row_at), (col_levels, col_at)):
+        for levels, at in ((col_levels, col_at), (row_levels, row_at)):
             if level < len(levels):
                 for k in levels[level]:
                     signal(entry_sem.at[level], at(k))
@@ -228,24 +228,6 @@
             edge_rows[i, k : k + 1, :] = line * edge
         rim_src[i, 0:16, :] = jnp.concatenate([row_src[1 * i], jnp.zeros((8, cols), F32)], axis=0).astype(BF16)
         rim_src[i, 16:32, :] = edge_rows[i].astype(BF16)
-    pl.semaphore_wait(barrier, len(row_first) + len(col_first))
-    halo = [
-        send(col_src.at[pl.ds(0, 8)], col_dst.at[pl.ds(8, 8)], halo_ssem.at[2], halo_rsem.at[2], left),
-        send(col_src.at[pl.ds(8, 8)], col_dst.at[pl.ds(0, 8)], halo_ssem.at[3], halo_rsem.at[3], right),
-    ]
-    told = tell(0)
-
-    rim_up = pltpu.make_async_remote_copy(
-        src_ref=rim_src.at[0], dst_ref=rim_dst.at[0], send_sem=rim_ssem.at[0], recv_sem=rim_rsem.at[0],
-        device_id=row_at((0, ys - 1)), device_id_type=MESH,
-    )
-
-    @pl.when(x == 0)
-    def _():
-        rim_up.start()
-
-    rim_right = send(rim_src.at[1], rim_dst.at[1], rim_ssem.at[1], rim_rsem.at[1], row_at((1, 0)))
-
     lane = iota((16, cols), 1)
     side = iota((16, cols), 0)
     zero_row = jnp.zeros((1, cols), F32)
@@ -269,20 +251,27 @@
     both = ones_where(((r16 < 8) & (c16 == 0)) | ((r16 >= 8) & (c16 == cols - 1)))
     coef_cols = mm(both, coef_high, NT) + mm(both, coef_low, NT)
 
-    hear(0, told)
-    told = tell(1)
-    halo += [
-        send(row_src.at[0], row_dst.at[1], halo_ssem.at[0], halo_rsem.at[0], up),
-        send(row_src.at[1], row_dst.at[0], halo_ssem.at[1], halo_rsem.at[1], down),
+    pl.semaphore_wait(barrier, len(row_first) + len(col_first))
+    told = tell(0)
+    halo = [
+        send(col_src.at[pl.ds(0, 8)], col_dst.at[pl.ds(8, 8)], halo_ssem.at[2], halo_rsem.at[2], left),
+        send(col_src.at[pl.ds(8, 8)], col_dst.at[pl.ds(0, 8)], halo_ssem.at[3], halo_rsem.at[3], right),
     ]
-    tan = []
-    for c in range(3):
-        tan.append(
-            (
-                send(inner.at[c, pl.ds(0, 64)], wide.at[c, pl.ds(192, 64)], tan_ssem.at[c, 0], tan_rsem.at[c, 0], up),
-                send(inner.at[c, pl.ds(64, 64)], wide.at[c, pl.ds(0, 64)], tan_ssem.at[c, 1], tan_rsem.at[c, 1], down),
-            )
-        )
+
+    @pl.when(x != 0)
+    def _():
+        rim_dst[0] = rim_src[0]
+
+    rim_up = pltpu.make_async_remote_copy(
+        src_ref=rim_src.at[0], dst_ref=rim_dst.at[0], send_sem=rim_ssem.at[0], recv_sem=rim_rsem.at[0],
+        device_id=row_at((0, ys - 1)), device_id_type=MESH,
+    )
+
+    @pl.when(x == 0)
+    def _():
+        rim_up.start()
+
+    rim_right = send(rim_src.at[1], rim_dst.at[1], rim_ssem.at[1], rim_rsem.at[1], row_at((1, 0)))
 
     l_basis.wait()
     r48 = iota((48, cols), 0)
@@ -305,14 +294,31 @@
     part = jnp.where((((cp // 16) % 3) == (rp // 16)) & (cp < 96), part, 0.0)
     sum1_src[...] = jnp.sum(part, axis=0, keepdims=True)
 
-    rb = iota((cols, cols), 0)
-    cb = iota((cols, cols), 1)
-    ends = ones_where(((rb == 0) & (cb < 128)) | ((rb == cols - 1) & (cb >= 128)))
-    lb = iota((rows, cols), 1)
-    edge_basis = jnp.zeros((rows, cols), F32)
+    rb = iota((32, cols), 0)
+    cb = iota((32, cols), 1)
+    edge_basis = jnp.zeros((32, rows), F32)
     for k in range(16):
-        edge_basis = jnp.where(lb % 16 == k, mm(basis[k], ends), edge_basis)
+        ends = ones_where(((rb == k) & (cb == 0)) | ((rb == 16 + k) & (cb == cols - 1)))
+        edge_basis = edge_basis + mm(ends, basis[k], NT)
     edge_basis = edge_basis.astype(BF16)
+    blank = jnp.zeros((32, rows), BF16)
+    first_basis = jnp.concatenate([edge_basis[0:16, :]] * 6 + [blank], axis=0)
+    last_basis = jnp.concatenate([edge_basis[16:32, :]] * 6 + [blank], axis=0)
+
+    hear(0, told)
+    told = tell(1)
+    halo += [
+        send(row_src.at[0], row_dst.at[1], halo_ssem.at[0], halo_rsem.at[0], up),
+        send(row_src.at[1], row_dst.at[0], halo_ssem.at[1], halo_rsem.at[1], down),
+    ]
+    tan = []
+    for c in range(3):
+        tan.append(
+            (
+                send(inner.at[c, pl.ds(0, 64)], wide.at[c, pl.ds(192, 64)], tan_ssem.at[c, 0], tan_rsem.at[c, 0], up),
+                send(inner.at[c, pl.ds(64, 64)], wide.at[c, pl.ds(0, 64)], tan_ssem.at[c, 1], tan_rsem.at[c, 1], down),
+            )
+        )
 
     halo[0].wait_recv()
     halo[1].wait_recv()
@@ -322,9 +328,6 @@
     shares_low = shares.astype(BF16)
     rh = iota((16, 128), 0)
     ch = iota((16, 128), 1)
-    part = jnp.where(rh < 8, mm(shares_low, edge_basis[:, 0:128]), mm(shares_low, edge_basis[:, 128:256]))
-    part = jnp.where(((ch // 16) % 3 == rh % 8) & (rh % 8 < 3) & (ch < 96), part, 0.0)
-    sum1_src[...] = sum1_src[...] + jnp.sum(part, axis=0, keepdims=True)
 
     for i in range(2):
         fix_src[i, 0:16, :] = shares
@@ -341,10 +344,6 @@
     def _():
         rim_up.wait_recv()
 
-    @pl.when(x != 0)
-    def _():
-        rim_dst[0] = rim_src[0]
-
     rim_right.wait_recv()
     upper = rim_dst[1]
     lower = rim_dst[0]
@@ -352,12 +351,14 @@
     edge = jnp.concatenate([lower[16:32, :], upper[16:32, :]], axis=1)
     edge = jnp.concatenate([edge] * 6 + [jnp.zeros((32, 2 * cols), BF16)], axis=0)
     inside = (x > 0) | (y < ys - 1)
-    part = jnp.where(((ch // 16) % 3 == rh) & (ch < 96) & inside, mm(values, edge, NT), 0.0)
-    sum1_src[...] = sum1_src[...] - jnp.sum(part, axis=0, keepdims=True)
+    across = jnp.where(inside, mm(values, edge, NT), 0.0)
+    part = jnp.where(rh < 8, mm(shares_low, first_basis, NT) - across, mm(shares_low, last_basis, NT))
+    part = jnp.where(((ch // 16) % 3 == rh % 8) & (rh % 8 < 3) & (ch < 96), part, 0.0)
+    sum1_src[...] = sum1_src[...] + jnp.sum(part, axis=0, keepdims=True)
+    for k in sorted(range(1, ncol), key=lambda k: (-ring(k, ncol), k)):
+        send(sum1_src, sum1_dst.at[k - 1], sum_ssem.at[0], sum_rsem.at[0], col_at(k))
     hear(1, told)
     told = tell(2)
-    for k in sorted(range(1, ncol), key=lambda k: (-ring(k, ncol), k)):
-        send(sum1_src, sum1_dst.at[k - 1], sum_ssem.at[0], sum_rsem.at[0], col_at(k))
 
     l_blk.wait()
     l_band.wait()
@@ -432,7 +433,6 @@
             )
         )
 
-    local(0)
 
     whole(sum1_dst, 0).wait_recv()
     sum2_src[...] = sum1_src[...] + jnp.sum(sum1_dst[...], axis=0)
@@ -441,6 +441,7 @@
         slot = offset[1] * xs + offset[0] - 1
         send(sum2_src, sum2_dst.at[slot], sum_ssem.at[1], sum_rsem.at[1], row_at(offset))
 
+    local(0)
     local(1)
     local(2)
 

time: 29.2 us -> 28.9 us (0.990)
  no operation moved by 1% of the time
where the time goes in v5:
time: 28.9 us; the launch traced here: 28.8 us
  Pallas kernels  27.4 us (95%)
  local copies, waits for them, and re-layouts  0.75 us (3%)
  between operations  0.66 us (2%)
    pallas_call x1, Pallas kernels, body(): pl.pallas_call(functools.partial(kernel, nrow, ncol), out_shape=vm((3, 12...  27.4 us
    unnamed x1, local copies, waits for them, and re-layouts  0.75 us

profile of v5, /device:TPU:1, one launch (start us, length us, event | category | flops | bytes accessed | tf_op | source)
XLA Modules:
  0.0 28.8 jit_solution(15495781544531773515)
XLA Ops:
  0.7 27.4 %schwarz.1 = f32[3,128,256]{2,1,0:T(8,128)S(1)} custom-call(f32[3,128,256]{2,1,0:T(8,128)} %dir_hbm.1, f32[3,128,256]{2,1,0:T(8,128)} %state_hbm.1, s32[128,256]{1,0:T(8,128)} %mat_hbm.1, s32[128,256]{1,0:T(8,128)} %trim_hbm.1, f32[8]{0:T(128)} %moduli_hbm.1, s32[1,1]{1,0:T(1,128)S(6)} %copy.12.band_hbm, bf16[1,1,3,256,256]{4,3,2,1,0:T(8,128)(2,1)} %blocks_hbm.1, ...), custom_call_target="tpu_custom_call" | custom-call | tf_op jit(solution)/shard_map/schwarz/pallas_call | solution.py:492
  28.0 0.7 %copy.11 = f32[3,128,256]{2,1,0:T(8,128)} copy(f32[3,128,256]{2,1,0:T(8,128)S(1)} %schwarz.1) | data formatting | bytes 786432

commit v6 on v5

--- a/solution.py
+++ b/solution.py
@@ -453,36 +453,33 @@
         own[c, 0:64, :] = own[c, 0:64, :] + res_dst[0, c].astype(F32)
         own[c, 64:128, :] = own[c, 64:128, :] + res_dst[1, c].astype(F32)
 
+    for copy in halo + fix + [rim_right]:
+        copy.wait_send()
+
+    @pl.when(x == 0)
+    def _():
+        rim_up.wait_send()
+
+    for c in range(3):
+        for copy in tan[c] + res[c]:
+            copy.wait_send()
+    whole(sum1_dst, 0).wait_send()
+
     whole(sum2_dst, 1).wait_recv()
     total = sum2_src[...] + jnp.sum(sum2_dst[...], axis=0)
     total = jnp.broadcast_to(total, (16, 128))
     high = total.astype(BF16).astype(F32)
     mid = (total - high).astype(BF16).astype(F32)
     low = total - high - mid
-    rt = iota((16, 128), 0)
-    split = jnp.where(rt == 0, high, jnp.where(rt == 1, mid, jnp.where(rt == 2, low, 0.0))).astype(BF16)
-    step = jnp.sum(mm(split, irep[...]), axis=0, keepdims=True)
-    step = step.astype(BF16).astype(F32)
-    spread = jnp.concatenate(
-        [jnp.broadcast_to(step[:, c * cols : c * cols + cols], (16, cols)) for c in range(3)], axis=0
-    )
+    step = mm(jnp.concatenate([high, mid, low], axis=0).astype(BF16), irep[...])
+    step = (step[0:16, :] + step[16:32, :] + step[32:48, :]).astype(BF16).astype(F32)
+    spread = jnp.concatenate([step[:, c * cols : c * cols + cols] for c in range(3)], axis=0)
     spread = jnp.where(same, spread, 0.0).astype(BF16)
     for g in range(groups):
         at = slice(16 * g, 16 * g + 16)
         term = mm(spread, basis[:, at, :].reshape(cols, cols))
         for c in range(3):
             out[c, at, :] = own[c, at, :] + term[16 * c : 16 * c + 16, :]
-    for copy in halo + fix + [rim_right]:
-        copy.wait_send()
-
-    @pl.when(x == 0)
-    def _():
-        rim_up.wait_send()
-
-    for c in range(3):
-        for copy in tan[c] + res[c]:
-            copy.wait_send()
-    whole(sum1_dst, 0).wait_send()
     whole(sum2_dst, 1).wait_send()
 
 

time: 28.9 us -> 28.9 us (level)
  no operation moved by 1% of the time
where the time goes in v6:
time: 28.9 us; the launch traced here: 28.8 us
  Pallas kernels  27.4 us (95%)
  local copies, waits for them, and re-layouts  0.75 us (3%)
  between operations  0.66 us (2%)
    pallas_call x1, Pallas kernels, body(): pl.pallas_call(functools.partial(kernel, nrow, ncol), out_shape=vm((3, 12...  27.4 us
    unnamed x1, local copies, waits for them, and re-layouts  0.75 us

profile of v6, /device:TPU:1, one launch (start us, length us, event | category | flops | bytes accessed | tf_op | source)
XLA Modules:
  0.0 28.8 jit_solution(9322370319683551770)
XLA Ops:
  0.7 27.4 %schwarz.1 = f32[3,128,256]{2,1,0:T(8,128)S(1)} custom-call(f32[3,128,256]{2,1,0:T(8,128)} %dir_hbm.1, f32[3,128,256]{2,1,0:T(8,128)} %state_hbm.1, s32[128,256]{1,0:T(8,128)} %mat_hbm.1, s32[128,256]{1,0:T(8,128)} %trim_hbm.1, f32[8]{0:T(128)} %moduli_hbm.1, s32[1,1]{1,0:T(1,128)S(6)} %copy.12.band_hbm, bf16[1,1,3,256,256]{4,3,2,1,0:T(8,128)(2,1)} %blocks_hbm.1, ...), custom_call_target="tpu_custom_call" | custom-call | tf_op jit(solution)/shard_map/schwarz/pallas_call | solution.py:489
  28.0 0.7 %copy.11 = f32[3,128,256]{2,1,0:T(8,128)} copy(f32[3,128,256]{2,1,0:T(8,128)S(1)} %schwarz.1) | data formatting | bytes 786432
